TPU v7x, 256 devices: a whole 4x4x8 slice. The times are simulated.
256 devices in a mesh: dp: 4 (over x), fsdp: 64 (over y, z, core).
Axes of the slice: x: 4, y: 4, z: 8, core: 2. Of those that a mesh axis runs over, the one named last changes fastest.
Arguments:
- hidden: bfloat16 [512, 4096], P('dp', 'fsdp'), may hold values from -6 to 6
- grad_query: bfloat16 [512, 4096], P('dp', 'fsdp'), may hold values from -6 to 6
- attn_out: bfloat16 [512, 4096], P('dp', 'fsdp'), may hold values from -6 to 6
- grad_output: bfloat16 [512, 4096], P('dp', 'fsdp'), may hold values from -6 to 6
- flat_params: float32 [33558528], P('fsdp')
- moment_one: float32 [33558528], P('fsdp'), may hold values from -192 to 192
- moment_two: float32 [33558528], P('fsdp'), may hold values from 20 to 400
- step_count: int32 [1], replicated, may hold values from 1 to 19
Outputs:
- grad_hidden: bfloat16 [512, 4096], P('dp', 'fsdp')
- grad_attn: bfloat16 [512, 4096], P('dp', 'fsdp')
- new_params: float32 [33558528], P('fsdp')
- new_moment_one: float32 [33558528], P('fsdp')
- new_moment_two: float32 [33558528], P('fsdp')
All inputs are finite; a program needn't handle non-finite values.
Results may differ from a plain program's by a relative error of at most 0.0012.
The roundings to bfloat16 on the way count: a program that leaves them out, or rounds other values in their place, can miss the bound.
Values may be sent and summed in bfloat16 or wider, within the bound.
A program may use at most 128 MiB of HBM per device.

v0:
```python
import math

import jax
import jax.numpy as jnp
from jax import lax
from jax.sharding import PartitionSpec as P

NHEAD = 32
HD = 128
D = 4096


beta_one = 0.9
beta_two = 0.95
adam_eps = 1e-08
learn_rate = 0.02
decay_rate = 0.1
lasso_weight = 2.0
norm_eps = 1e-06


def window_of(values, lead_cells, window_rows):
    buffer = jnp.zeros((window_rows * D,), values.dtype)
    buffer = lax.dynamic_update_slice(buffer, values, (lead_cells,))
    return buffer.reshape(window_rows, D)


def shard_of(window, lead_cells, shard_len):
    return lax.dynamic_slice(window.reshape(-1), (lead_cells,), (shard_len,))


def left_window(query_all, output_all, first_row, window_rows):
    tokens_here = query_all.shape[0]
    gap_col = jnp.zeros((tokens_here, 1), query_all.dtype)
    padding = jnp.zeros((tokens_here, window_rows), query_all.dtype)
    joined = jnp.concatenate([query_all, gap_col, output_all, padding], axis=1)
    return lax.dynamic_slice(joined, (jnp.int32(0), first_row), (tokens_here, window_rows))


def weight_grads(left_win, hidden_all, attn_all, is_query, is_output, row_kind):
    contract = (((0,), (0,)), ((), ()))

    def only_query():
        product = lax.dot_general(
            left_win, hidden_all, contract, preferred_element_type=jnp.float32
        )
        return jnp.where(is_query[:, None], product, 0.0)

    def only_output():
        product = lax.dot_general(left_win, attn_all, contract, preferred_element_type=jnp.float32)
        return jnp.where(is_output[:, None], product, 0.0)

    def both_parts():
        return only_query() + only_output()

    return lax.switch(row_kind, (only_query, only_output, both_parts))


def on_device(
    hidden, grad_query, attn_out, grad_output, flat_params, moment_one, moment_two, step_count
):
    hidden_all, query_all, attn_all, output_all = (
        lax.all_gather(hidden, "fsdp", axis=1, tiled=True),
        lax.all_gather(grad_query, "fsdp", axis=1, tiled=True),
        lax.all_gather(attn_out, "fsdp", axis=1, tiled=True),
        lax.all_gather(grad_output, "fsdp", axis=1, tiled=True),
    )
    shard_len = flat_params.shape[0]
    window_rows = (shard_len // D + 2 + 127) // 128 * 128
    offset = lax.axis_index("fsdp") * shard_len
    first_row = offset // D
    lead_cells = offset - first_row * D
    last_row = (offset + shard_len - 1) // D
    row_kind = jnp.where(last_row < D, 0, jnp.where(first_row >= D, 1, 2)).astype(jnp.int32)
    row_ids = first_row + jnp.arange(window_rows, dtype=jnp.int32)
    is_query = row_ids < D
    is_bias = row_ids == D
    is_output = (row_ids > D) & (row_ids <= 2 * D)
    own_left = left_window(query_all, output_all, first_row, window_rows)
    every_left, every_hidden, every_attn = (
        lax.all_gather(own_left, "dp", axis=0, tiled=True),
        lax.all_gather(hidden_all, "dp", axis=0, tiled=True),
        lax.all_gather(attn_all, "dp", axis=0, tiled=True),
    )
    bias_sum = lax.psum(jnp.sum(query_all, axis=0, dtype=jnp.float32), "dp")
    grad_win = weight_grads(every_left, every_hidden, every_attn, is_query, is_output, row_kind)
    grad_win = grad_win + jnp.where(is_bias[:, None], bias_sum[None, :], 0.0)
    gradient = shard_of(grad_win, lead_cells, shard_len)
    weight_win = window_of(flat_params, lead_cells, window_rows)
    query_rows = jnp.where(is_query[:, None], weight_win, 0.0).astype(jnp.bfloat16)
    output_rows = jnp.where(is_output[:, None], weight_win, 0.0).astype(jnp.bfloat16)
    contract = (((0,), (1,)), ((), ()))
    to_hidden = lax.dot_general(query_rows, own_left, contract, preferred_element_type=jnp.float32)
    to_attn = lax.dot_general(output_rows, own_left, contract, preferred_element_type=jnp.float32)
    summed = lax.psum_scatter(
        jnp.concatenate([to_hidden, to_attn], axis=1), "fsdp", scatter_dimension=0, tiled=True
    )
    tokens_here = hidden.shape[0]
    grad_hidden = summed[:, :tokens_here].T.astype(jnp.bfloat16)
    grad_attn = summed[:, tokens_here:].T.astype(jnp.bfloat16)
    step_num = step_count[0].astype(jnp.float32)
    new_one = beta_one * moment_one + (1.0 - beta_one) * gradient
    new_two = beta_two * moment_two + (1.0 - beta_two) * gradient * gradient
    first_fix = 1.0 - jnp.power(jnp.float32(beta_one), step_num)
    second_fix = 1.0 - jnp.power(jnp.float32(beta_two), step_num)
    direction = new_one / first_fix / (jnp.sqrt(new_two / second_fix) + adam_eps)
    updated = flat_params - learn_rate * (direction + decay_rate * flat_params)
    updated_win = window_of(updated, lead_cells, window_rows)
    squares = updated_win * updated_win
    row_sums = jnp.sum(jnp.where(is_query[:, None], squares, 0.0), axis=1)
    head_ids = jnp.arange(NHEAD, dtype=jnp.int32)
    member = (row_ids // HD)[:, None] == head_ids[None, :]
    from_rows = jnp.sum(jnp.where(member, row_sums[:, None], 0.0), axis=0)
    col_sums = jnp.sum(jnp.where(is_query[:, None], 0.0, squares), axis=0)
    from_cols = jnp.sum(col_sums.reshape(NHEAD, HD), axis=1)
    sumsq = lax.psum(from_rows + from_cols, "fsdp")
    head_norm = jnp.sqrt(sumsq + norm_eps)
    threshold = learn_rate * lasso_weight * math.sqrt(2 * HD * D + HD)
    shrink = jnp.maximum(1.0 - threshold / head_norm, 0.0)
    row_shrink = jnp.sum(jnp.where(member, shrink[None, :], 0.0), axis=1)
    col_shrink = jnp.repeat(shrink, HD)
    shrink_win = jnp.where(is_query[:, None], row_shrink[:, None], col_shrink[None, :])
    new_params = shard_of(updated_win * shrink_win, lead_cells, shard_len)
    return (grad_hidden, grad_attn, new_params, new_one, new_two)


def solution(mesh):
    in_specs = (
        P("dp", "fsdp"),
        P("dp", "fsdp"),
        P("dp", "fsdp"),
        P("dp", "fsdp"),
        P("fsdp"),
        P("fsdp"),
        P("fsdp"),
        P(),
    )
    out_specs = (P("dp", "fsdp"), P("dp", "fsdp"), P("fsdp"), P("fsdp"), P("fsdp"))
    return jax.shard_map(
        on_device, mesh=mesh, in_specs=in_specs, out_specs=out_specs, check_vma=False
    )
```

profile of v0, /device:TPU:1, one launch (start us, length us, event | category | flops | bytes accessed | tf_op | source)
XLA Modules:
  0.0 624.4 jit_solution(4305664683217453073)
XLA Ops:
  7.2 0.0 copy-start.2
  7.2 0.0 all-gather.15.cloned.1.call-start
  7.2 0.7 all-gather.15.cloned.1.call-update
  7.9 0.0 all-gather.11.cloned.1.call-start
  8.0 0.7 all-gather.11.cloned.1.call-update
  8.7 0.0 all-gather.7.cloned.1.call-start
  8.7 0.7 all-gather.7.cloned.1.call-update
  9.4 0.0 all-gather.9.cloned.1.call-start
  9.4 0.5 all-gather.9.cloned.1.call-update
  10.0 0.0 all-gather.17.cloned.1.call-start
  10.0 81.4 %all-gather.15.cloned.1.call-done = bf16[128,4096]{0,1:T(8,128)(2,1)} async-done(((bf16[128,64]{0,1:T(8,128)(2,1)}), bf16[128,4096]{0,1:T(8,128)(2,1)}) %all-gather.15.cloned.1.call-update) | async-done | bytes 1048592 | tf_op jit(solution)/shard_map/all_gather | solution.py:65
  91.5 0.0 all-gather.17.cloned.1.call-update
  91.5 0.0 all-gather.13.cloned.1.call-start
  91.5 76.8 %all-gather.11.cloned.1.call-done = bf16[128,4096]{0,1:T(8,128)(2,1)} async-done(((bf16[128,64]{0,1:T(8,128)(2,1)}), bf16[128,4096]{0,1:T(8,128)(2,1)}) %all-gather.11.cloned.1.call-update) | async-done | bytes 1048592 | tf_op jit(solution)/shard_map/all_gather | solution.py:63
  168.3 0.0 all-gather.13.cloned.1.call-update
  168.4 0.0 reduce-scatter.4.cloned.1.call-start
  169.2 2.2 broadcast.86.clone
  171.4 0.0 copy-done.2
  171.4 18.1 %dynamic_update_slice.6 = f32[1048576]{0:T(1024)} dynamic-update-slice(f32[1048576]{0:T(1024)} %broadcast.86.clone, f32[524352]{0:T(1024)S(1)} %copy-done.2, s32[]{:T(128)S(6)} %select_n.81) | dynamic-update-slice | bytes 4194820 | tf_op jit(solution)/shard_map/dynamic_update_slice | solution.py:24
  189.5 3.3 reshape.74
  192.8 52.5 %all-gather.7.cloned.1.call-done = bf16[128,4096]{0,1:T(8,128)(2,1)} async-done(((bf16[128,64]{0,1:T(8,128)(2,1)}), bf16[128,4096]{0,1:T(8,128)(2,1)}) %all-gather.7.cloned.1.call-update) | async-done | bytes 1048592 | tf_op jit(solution)/shard_map/all_gather | solution.py:64
  245.3 76.7 %all-gather.9.cloned.1.call-done = bf16[128,4096]{0,1:T(8,128)(2,1)} async-done(((bf16[128,64]{0,1:T(8,128)(2,1)}), bf16[128,4096]{0,1:T(8,128)(2,1)}) %all-gather.9.cloned.1.call-update) | async-done | bytes 1048592 | tf_op jit(solution)/shard_map/all_gather | solution.py:66
  322.1 13.1 %concatenate.6 = bf16[128,8449]{0,1:T(8,128)(2,1)} concatenate(bf16[128,4096]{0,1:T(8,128)(2,1)} %all-gather.7.cloned.1.call-done, bf16[128,1]{0,1:T(2,128)(2,1)S(1)} %broadcast_in_dim.151, bf16[128,4096]{0,1:T(8,128)(2,1)} %all-gather.9.cloned.1.call-done, bf16[128,256]{0,1:T(8,128)(2,1)S(1)} %broadcast_in_dim.152), dimensions={1} | concatenate | bytes 4325888 | tf_op jit(solution)/shard_map/concatenate | solution.py:36
  335.1 0.9 constant_dynamic-slice_fusion
  336.1 0.5 fusion.3
  336.6 0.5 fusion.2
  337.1 2.4 pad_maximum_fusion
  339.5 5.7 copy.44
  345.2 0.0 copy-done.4
  345.2 0.3 convert_reduce_fusion
  345.6 14.5 %psum.14 = f32[4096]{0:T(1024)S(1)} all-reduce(f32[4096]{0:T(1024)S(1)} %convert_reduce_fusion), channel_id=1, replica_groups=mesh['dp'=4,'fsdp'=64] {'dp'}, use_global_device_ids=true, to_apply=%region_5.6 | all-reduce | flops 4096 | bytes 32768 | tf_op jit(solution)/shard_map/psum | solution.py:85
  360.1 11.7 %all_gather.23 = bf16[512,256]{0,1:T(8,128)(2,1)S(1)} all-gather(bf16[128,256]{0,1:T(8,128)(2,1)S(1)} %constant_dynamic-slice_fusion), channel_id=1, replica_groups=mesh['dp'=4,'fsdp'=64] {'dp'}, dimensions={0}, use_global_device_ids=true | all-gather | bytes 327680 | tf_op jit(solution)/shard_map/all_gather | solution.py:81
  371.8 0.0 reduce-scatter.4.cloned.1.call-update
  371.8 6.7 %all-gather.17.cloned.1.call-done = bf16[512,4096]{0,1:T(8,128)(2,1)} async-done(((bf16[128,4096]{0,1:T(8,128)(2,1)}), bf16[512,4096]{0,1:T(8,128)(2,1)}) %all-gather.17.cloned.1.call-update) | async-done | bytes 4194320 | tf_op jit(solution)/shard_map/all_gather | solution.py:83
  378.5 55.9 %all-gather.13.cloned.1.call-done = bf16[512,4096]{0,1:T(8,128)(2,1)} async-done(((bf16[128,4096]{0,1:T(8,128)(2,1)}), bf16[512,4096]{0,1:T(8,128)(2,1)}) %all-gather.13.cloned.1.call-update) | async-done | bytes 4194320 | tf_op jit(solution)/shard_map/all_gather | solution.py:82
  434.4 5.4 conditional.1
  434.4 5.4 convolution_select_fusion
  439.8 2.7 add_bitcast_fusion
  442.6 0.0 copy-start.3
  442.6 0.0 copy-start.5
  442.6 0.0 copy-start.6
  442.6 0.8 copy.46
  443.4 0.8 copy-done.3
  444.2 0.6 copy-done.5
  444.8 0.6 copy-done.6
  445.4 4.0 multiply_subtract_fusion
  449.4 2.2 broadcast.86.clone.1
  451.7 18.1 %dynamic_update_slice.7 = f32[1048576]{0:T(1024)} dynamic-update-slice(f32[1048576]{0:T(1024)} %broadcast.86.clone.1, f32[524352]{0:T(1024)S(1)} %get-tuple-element.81, s32[]{:T(128)S(6)} %select_n.81) | dynamic-update-slice | bytes 4194820 | tf_op jit(solution)/shard_map/dynamic_update_slice | solution.py:24
  469.8 6.0 mul.62
  475.8 5.0 mul.63
  480.8 3.0 select_reduce_fusion
  483.8 0.1 bitcast_reduce_fusion
  483.9 0.1 select_reduce_fusion.3
  484.0 125.9 %psum.15 = f32[32]{0:T(128)S(1)} all-reduce(f32[32]{0:T(128)S(1)} %add.85), channel_id=1, replica_groups=mesh['dp'=4,'fsdp'=64] {'fsdp'}, use_global_device_ids=true, to_apply=%region_10.11 | all-reduce | flops 32 | bytes 256 | tf_op jit(solution)/shard_map/psum | solution.py:116
  609.9 0.1 select_reduce_fusion.2
  610.0 0.1 broadcast_bitcast_fusion
  610.1 1.0 copy.45
  611.0 0.7 copy.36
  611.7 0.7 copy.35
  612.4 0.5 select_bitcast_fusion
  612.9 0.0 copy-start
  612.9 0.8 copy.47
  613.7 1.4 copy-done
  615.1 2.5 dynamic-slice_multiply_fusion
  (10 shorter events, 0.1 us)
Async XLA Ops:
  7.2 164.2 %copy-start.2 = (f32[524352]{0:T(1024)S(1)}, f32[524352]{0:T(1024)}, u32[]{:S(2)}) copy-start(f32[524352]{0:T(1024)} %param.15) | copy-start | bytes 6292228
  7.2 84.3 %all-gather.15.cloned.1.call-start = ((), (), s32[]{:S(2)}) async-start(), calls=%async_computation.5 | async-start | bytes 1064960 | tf_op jit(solution)/shard_map/all_gather | solution.py:65
  7.9 160.4 %all-gather.11.cloned.1.call-start = ((), (), s32[]{:S(2)}) async-start(), calls=%async_computation.3 | async-start | bytes 1064960 | tf_op jit(solution)/shard_map/all_gather | solution.py:63
  8.7 236.6 %all-gather.7.cloned.1.call-start = ((), (), s32[]{:S(2)}) async-start(), calls=%async_computation.1 | async-start | bytes 1064960 | tf_op jit(solution)/shard_map/all_gather | solution.py:64
  9.4 312.6 %all-gather.9.cloned.1.call-start = ((), (), s32[]{:S(2)}) async-start(), calls=%async_computation.2 | async-start | bytes 1064960 | tf_op jit(solution)/shard_map/all_gather | solution.py:66
  10.0 368.5 %all-gather.17.cloned.1.call-start = ((), (), s32[]{:S(2)}) async-start(), calls=%async_computation.6 | async-start | bytes 5242880 | tf_op jit(solution)/shard_map/all_gather | solution.py:83
  91.5 342.9 %all-gather.13.cloned.1.call-start = ((), (), s32[]{:S(2)}) async-start(), calls=%async_computation.4 | async-start | bytes 5242880 | tf_op jit(solution)/shard_map/all_gather | solution.py:82
  168.4 441.7 %reduce-scatter.4.cloned.1.call-start = ((), (), s32[]{:S(2)}) async-start(), calls=%async_computation.7 | async-start | bytes 4259840
  339.5 5.7 copy-start.4
  442.6 1.6 copy-start.3
  442.6 2.2 copy-start.5
  442.6 2.8 copy-start.6
  612.9 2.2 copy-start
Sparse Core Ops, SparseCore 0:
  10.8 80.6 all-gather.14
  94.2 74.0 all-gather.10
  171.1 74.1 all-gather.6
  247.9 74.0 all-gather.8
  323.7 54.7 all-gather.16
  380.1 54.2 all-gather.12
  438.5 141.2 reduce-scatter.3
where the time goes:
time: 630 us; the launch traced here: 624 us
  waiting for transfers between devices  353 us (56%)
  blocking collectives  152 us (24%)
  local copies, waits for them, and re-layouts  76.1 us (12%)
  other arithmetic  21.8 us (3%)
  between operations  15.1 us (2%)
  matrix products  6.47 us (1%)
    psum x1, blocking collectives, on_device(): sumsq = lax.psum(from_rows + from_cols, 'fsdp')  126 us
    all_gather x1, waiting for transfers between devices, on_device(): lax.all_gather(attn_out, 'fsdp', axis=1, tiled=True)  81.4 us
    all_gather x1, waiting for transfers between devices, on_device(): lax.all_gather(hidden, 'fsdp', axis=1, tiled=True)  76.8 us
    all_gather x1, waiting for transfers between devices, on_device(): lax.all_gather(grad_output, 'fsdp', axis=1, tiled=True)  76.7 us
    all_gather x1, waiting for transfers between devices, on_device(): lax.all_gather(hidden_all, 'dp', axis=0, tiled=True)  55.9 us
    all_gather x1, waiting for transfers between devices, on_device(): lax.all_gather(grad_query, 'fsdp', axis=1, tiled=True)  52.5 us
    dynamic_update_slice x2, local copies, waits for them, and re-layouts, window_of(): buffer = lax.dynamic_update_slice(buffer, values, (lead_cells,))  36.2 us
    psum x1, blocking collectives, on_device(): bias_sum = lax.psum(jnp.sum(query_all, axis=0, dtype=jnp.float32), 'dp')  14.5 us
  transfers between devices with their start and end apart: 7, of which 6 were waited for; matrix products, arithmetic and copies ran while one was open for 15% of the time, Pallas kernels for 0%

commit v1 on v0

v1 whole, which is shorter than its diff:
```python
import functools
import math

import jax
import jax.numpy as jnp
from jax import lax
from jax.experimental import pallas as pl
from jax.experimental.pallas import tpu as pltpu
from jax.sharding import PartitionSpec as P

HD = 128
NX = 4
NY = 4
CORES = 2
TOK = 128
BLK = 128

beta_one = 0.9
beta_two = 0.95
adam_eps = 1e-08
learn_rate = 0.02
decay_rate = 0.1
lasso_weight = 2.0
norm_eps = 1e-06

MESH = pl.DeviceIdType.MESH
F32 = jnp.float32
BF16 = jnp.bfloat16
NT = (((1,), (1,)), ((), ()))


def kernel(
    nz, hb, gb, ab, ob, tails, fixes, p_hbm, m1_hbm, m2_hbm,
    gh_out, ga_out, np_out, n1_out, n2_out,
    p1, m1, m2, p2, o1, o2, g2, gw,
    pack, rpack, xblk, lsend, lb, rg, lt, ll, lown,
    rbuf, pb, xs, xr, ring, yb, bias_own, bias_grp, bias_got,
    ext_ref, acc_ref, last_ref, s_own, s_grp, s_mid, s_col,
    in_sem, out_sem, s_sw, r_sw, s_ry, r_ry, s_lf, r_lf, s_lx, r_lx,
    s_bg, r_bg, s_by, r_by, s_rz, r_rz, s_r1, r_r1, s_r2, r_r2, s_rp, r_rp,
    s_sp, r_sp, s_sr, r_sr, s_sy, r_sy, s_sg, r_sg, s_ss, r_ss,
):
    nf = NY * nz * CORES
    nb = NY * nz
    dim = nb * BLK
    half_y = NY // 2
    longs, shorts = nz // 2, nz - 1 - nz // 2
    x = lax.axis_index("dp")
    f = lax.axis_index("fsdp")
    c = f % CORES
    z = (f // CORES) % nz
    y = f // (CORES * nz)
    h = y // half_y
    m = f // 2
    par = f % 2
    k = f // CORES
    sig = 1 - 2 * c

    def fid(yy, zz, cc):
        return (yy * nz + zz) * CORES + cc

    def zw(v):
        return (v + 2 * nz) % nz

    partner = fid(y, z, 1 - c)
    z_long = fid(y, zw(z + sig), c)
    z_short = fid(y, zw(z - sig), c)
    x_up = (x + 1) % NX
    x_down = (x + NX - 1) % NX
    x_far = (x + 2) % NX

    pending = []

    def send(src, dst, ss, rs, xx, ff):
        copy = pltpu.make_async_remote_copy(
            src_ref=src, dst_ref=dst, send_sem=ss, recv_sem=rs,
            device_id=(xx, ff), device_id_type=MESH,
        )
        copy.start()
        return copy

    def send_later(*args):
        pending.append(send(*args))

    def arrive(dst, rs):
        pltpu.make_async_remote_copy(
            src_ref=dst, dst_ref=dst, send_sem=s_sw, recv_sem=rs,
            device_id=(x, partner), device_id_type=MESH,
        ).wait_recv()

    cells = nb * BLK * BLK
    loads = [
        pltpu.make_async_copy(src.at[pl.ds(0, cells)], dst, in_sem.at[i])
        for i, (src, dst) in enumerate(((p_hbm, p1), (m1_hbm, m1), (m2_hbm, m2)))
    ]
    for load in loads:
        load.start()

    barrier = pltpu.get_barrier_semaphore()

    def greet(xx, ff):
        pl.semaphore_signal(barrier, inc=1, device_id=(xx, ff), device_id_type=MESH)

    group = [(dz, dc) for dz in range(nz) for dc in range(CORES) if (dz, dc) != (0, 0)]
    for dz, dc in group:
        greet(x, fid(y, zw(z + dz), (c + dc) % CORES))
    for dy in range(1, NY):
        for dc in range(CORES):
            greet(x, fid((y + dy) % NY, z, (c + dc) % CORES))
    for dx in range(1, NX):
        greet((x + dx) % NX, f)
    fl = f % (nf // 2)
    left_src = 2 * fl + h
    row_src = 2 * (fl + 1 - 2 * h) + h
    row_chip = fl + 1 - 2 * h
    has_row = (row_chip >= 0) & (row_chip < nf // 2)
    left_dst = c * (nf // 2) + k
    row_dst_low = k - 1 + 2 * c
    gives_row = (row_dst_low >= 0) & (row_dst_low < nf // 2)
    row_dst = c * (nf // 2) + row_dst_low

    @pl.when(left_src != f)
    def _():
        greet(x, left_src)

    @pl.when(has_row)
    def _():
        greet(x, row_src)

    own_pack = jnp.where(
        c == 0,
        jnp.concatenate([hb[...], gb[...]], axis=1).astype(F32),
        jnp.concatenate([ab[...], ob[...]], axis=1).astype(F32),
    )
    pack[...] = jnp.where(
        c == 0,
        jnp.concatenate([ab[...], ob[...]], axis=1).astype(F32),
        jnp.concatenate([hb[...], gb[...]], axis=1).astype(F32),
    ).astype(BF16)

    greeted = len(group) + (NY - 1) * CORES + NX - 1
    greeted = greeted + (left_dst != f).astype(jnp.int32) + gives_row.astype(jnp.int32)
    pl.semaphore_wait(barrier, greeted)

    send_later(pack, rpack, s_sw, r_sw, x, partner)
    lane = lax.broadcasted_iota(jnp.int32, (BLK, BLK), 1)
    row = lax.broadcasted_iota(jnp.int32, (BLK, BLK), 0)
    low = lane < 64
    arrive(rpack, r_sw)
    got = rpack[...].astype(F32)
    even = jnp.where(c == 0, own_pack, got)
    odd = jnp.where(c == 0, got, own_pack)
    right = jnp.where(low, even, pltpu.roll(odd, 64, 1))
    left = jnp.where(low, pltpu.roll(even, 64, 1), odd)
    xblk[...] = right.astype(BF16)

    for i in range(half_y):
        for cc in range(CORES):
            yd = half_y * c + i

            @pl.when((yd != y) | (cc != c))
            def _(i=i, cc=cc, yd=yd):
                send(xblk, rbuf.at[x, z, y], s_ry.at[i, cc], r_ry.at[y], x, fid(yd, z, cc))

    @pl.when(h == c)
    def _():
        rbuf[x, z, y] = right.astype(BF16)

    left_t = jnp.transpose(left)
    lsend[...] = left_t.astype(BF16)

    @pl.when(left_dst != f)
    def _():
        send(lsend, lb.at[x], s_lf.at[0], r_lf.at[0], x, left_dst)

    @pl.when(left_dst == f)
    def _():
        lb[x] = left_t.astype(BF16)

    @pl.when(gives_row)
    def _():
        send(
            lsend.at[pl.ds(pl.multiple_of(c * (BLK - 16), 16), 16)],
            rg.at[x], s_lf.at[1], r_lf.at[1], x, row_dst,
        )

    @pl.when(jnp.logical_not(has_row))
    def _():
        rg[x] = jnp.zeros((16, TOK), BF16)

    loads[0].wait()
    step_cells = 8 * dim

    @pl.loop(0, BLK // 8)
    def _(i):
        p2[pl.ds(i * 8 * nb, 8 * nb), :] = p1[pl.ds(i * step_cells, step_cells)].reshape(8 * nb, BLK)

    pair = lambda cc: pl.ds(half_y * cc, half_y)
    for yy in range(NY):

        @pl.when((yy != y) | (h != c))
        def _(yy=yy):
            arrive(rbuf.at[x, z, yy], r_ry.at[yy])

    def z_quad(r):
        out = []
        if r == 0:
            return [(0, z)]
        if r <= longs:
            out.append((2 * r - 1, zw(z - sig * r)))
        if r <= shorts:
            out.append((2 * r, zw(z + sig * r)))
        return out

    def round_a(r):
        for idx, zq in z_quad(r):
            ref = rbuf.at[x, zq, pair(c)]
            if r > 0:
                arrive(ref, r_rz.at[idx])
            is_long = r == 0 or idx % 2 == 1
            is_short = r == 0 or idx % 2 == 0
            if is_long and r < longs:
                send_later(ref, ref, s_rz.at[2 * r + 1], r_rz.at[2 * r + 1], x, z_long)
            if is_short and r < shorts:
                send_later(ref, ref, s_rz.at[2 * r + 2], r_rz.at[2 * r + 2], x, z_short)
            send_later(ref, ref, s_r1.at[idx, 0], r_r1.at[idx, 0], x_up, f)
            send_later(ref, ref, s_r1.at[idx, 1], r_r1.at[idx, 1], x_down, f)
            if r > 0:
                send_later(ref, ref, s_rp.at[x, zq], r_rp.at[x, zq], x, partner)

    def round_x1(r):
        for idx, zq in z_quad(r):
            for way, (frm, to) in enumerate(((x_down, x_up), (x_up, x_down))):
                ref = rbuf.at[frm, zq, pair(c)]
                arrive(ref, r_r1.at[idx, way])
                part = rbuf.at[frm, zq, half_y * c + way]
                send_later(part, part, s_r2.at[idx, way], r_r2.at[idx, way], to, f)
                send_later(ref, ref, s_rp.at[frm, zq], r_rp.at[frm, zq], x, partner)

    def round_x2(r):
        for idx, zq in z_quad(r):
            for way in range(2):
                arrive(rbuf.at[x_far, zq, half_y * c + way], r_r2.at[idx, way])
            ref = rbuf.at[x_far, zq, pair(c)]
            send_later(ref, ref, s_rp.at[x_far, zq], r_rp.at[x_far, zq], x, partner)

    round_a(0)

    @pl.when(left_src != f)
    def _():
        arrive(lb.at[x], r_lf.at[0])

    @pl.when(has_row)
    def _():
        arrive(rg.at[x], r_lf.at[1])

    for dx in range(1, NX):
        xx = (x + dx) % NX
        send_later(lb.at[x], lb.at[x], s_lx.at[dx - 1, 0], r_lx.at[x, 0], xx, f)
        send_later(rg.at[x], rg.at[x], s_lx.at[dx - 1, 1], r_lx.at[x, 1], xx, f)

    def build_left(xx):
        lt[pl.ds(0, 16), :] = rg[xx].astype(F32)
        lt[pl.ds(16, BLK), :] = lb[xx].astype(F32)
        lt[pl.ds(16 + BLK, 16), :] = rg[xx].astype(F32)
        before = lt[pl.ds(15, BLK), :]
        middle = lt[pl.ds(16, BLK), :]
        after = lt[pl.ds(17, BLK), :]
        zero = jnp.where(h == 0, middle, before)
        one = jnp.where(h == 0, after, middle)
        return zero, one

    zero, one = build_left(x)
    lown[:, pl.ds(0, BLK)] = jnp.transpose(zero).astype(BF16)
    lown[:, pl.ds(BLK, BLK)] = jnp.transpose(one).astype(BF16)

    tail_p = tails[pl.ds(0, 1), :]
    tail_here = jnp.where(par == 1, pltpu.roll(tails[...], 64, 1)[0:1], tail_p)

    def window_block(j):
        first = p2[pl.ds((j - m + nb) % nb, BLK, stride=nb), :]
        second = p2[pl.ds((j - m - 1 + nb) % nb, BLK, stride=nb), :]
        mixed = pltpu.roll(jnp.where(low, first, second), 64, 1)
        block = jnp.where(par == 1, mixed, first)
        column = j * BLK + lane
        carried = column < 64 * f
        top = jnp.where(carried, 0.0, block)
        bottom = jnp.where(carried, block, 0.0)
        is_tail = (row == BLK - 1) & (column >= 64 * f) & (column < 64 * f + 64)
        bottom = jnp.where(is_tail, tail_here, bottom)
        return jnp.concatenate([top, bottom], axis=0).astype(BF16)

    def partial_chunk(d):
        for mine in range(2):
            hh = c if mine == 0 else 1 - c
            wide = jnp.concatenate(
                [window_block((half_y * hh + i) * nz + d) for i in range(half_y)], axis=1
            )
            part = jnp.dot(lown[...], wide, preferred_element_type=F32)
            for i in range(half_y):
                target = pb if mine == 0 else xs
                target[d, i] = part[:, i * BLK : (i + 1) * BLK]
        send_later(xs.at[d], xr.at[d], s_sp.at[d], r_sp.at[d], x, partner)

    def round_c(r):
        if r >= longs:
            return
        partial_chunk(zw(z + sig * (longs - r)))
        partial_chunk(zw(z - sig * (shorts - r)))

    def chip_sum(d):
        arrive(xr.at[d], r_sp.at[d])
        return pb[d] + xr[d]

    def round_e(r):
        for way, (hops, to, sign) in enumerate(((longs, z_long, 1), (shorts, z_short, -1))):
            if r >= hops:
                continue
            d = zw(z + sig * sign * (hops - r))
            slot = 2 * r + way
            if r == 0:
                pb[d] = chip_sum(d)
                src = pb.at[d]
            else:
                before = slot - 2
                arrive(ring.at[before], r_sr.at[before])
                ring[before] = ring[before] + chip_sum(d)
                src = ring.at[before]
            send_later(src, ring.at[slot], s_sr.at[slot], r_sr.at[slot], x, to)

    def finish_sums():
        total = chip_sum(z)
        slot = 2 * (longs - 1)
        arrive(ring.at[slot], r_sr.at[slot])
        total = total + ring[slot]
        if shorts:
            slot = 2 * (shorts - 1) + 1
            arrive(ring.at[slot], r_sr.at[slot])
            total = total + ring[slot]
        pb[z] = total
        for i in range(half_y):
            for cc in range(CORES):
                yd = half_y * c + i

                @pl.when((yd != y) | (cc != c))
                def _(i=i, cc=cc, yd=yd):
                    send(pb.at[z, i], yb.at[y], s_sy.at[i, cc], r_sy.at[y], x, fid(yd, z, cc))

        @pl.when(h == c)
        def _():
            yb[y] = pb[z, y % half_y]

    def write_cotangents():
        for yy in range(NY):

            @pl.when((yy != y) | (h != c))
            def _(yy=yy):
                arrive(yb.at[yy], r_sy.at[yy])

        for out, base_y in ((gh_out, 0), (ga_out, half_y)):
            total = yb[base_y]
            for i in range(1, half_y):
                total = total + yb[base_y + i]
            total = jnp.where(c == 1, pltpu.roll(total, 64, 1), total)
            out[...] = total[:, :64].astype(BF16)

    def full_left():
        for xx in range(NX):

            @pl.when(xx != x)
            def _(xx=xx):
                arrive(lb.at[xx], r_lx.at[xx, 0])
                arrive(rg.at[xx], r_lx.at[xx, 1])

            zero, one = build_left(xx)
            ll[pl.ds(0, BLK), pl.ds(xx * TOK, TOK)] = zero.astype(BF16)
            ll[pl.ds(BLK, BLK), pl.ds(xx * TOK, TOK)] = one.astype(BF16)
        bias_own[...] = lax.dot_general(
            jnp.ones((8, NX * TOK), BF16), ll[pl.ds(0, BLK), :], NT, preferred_element_type=F32
        )
        me = z * CORES + c
        bias_grp[me] = bias_own[...]
        for i, (dz, dc) in enumerate(group):
            zz, cc = zw(z + dz), (c + dc) % CORES
            send_later(bias_own, bias_grp.at[me], s_bg.at[i], r_bg.at[me], x, fid(y, zz, cc))

    def bias_on():
        for dz, dc in group:
            other = zw(z + dz) * CORES + (c + dc) % CORES
            arrive(bias_grp.at[other], r_bg.at[other])
        send_later(bias_grp, bias_got, s_by, r_by, x, fid((y + 1) % NY, z, c))

    ext_ref[...] = jnp.zeros((8, BLK), F32)

    def gradient_quad(r):
        for _, zq in z_quad(r):
            for xx in range(NX):
                if r == 0:

                    @pl.when(xx != x)
                    def _(xx=xx, zq=zq):
                        arrive(rbuf.at[xx, zq, pair(1 - c)], r_rp.at[xx, zq])
                else:
                    arrive(rbuf.at[xx, zq, pair(1 - c)], r_rp.at[xx, zq])
            for yy in range(0, NY, 2):
                wide = jnp.concatenate(
                    [
                        jnp.concatenate([rbuf[xx, zq, yy], rbuf[xx, zq, yy + 1]], axis=1)
                        for xx in range(NX)
                    ],
                    axis=0,
                )
                both = jnp.dot(ll[...], wide, preferred_element_type=F32)
                for i in range(2):
                    j = (yy + i) * nz + zq
                    p_zero = both[:BLK, i * BLK : (i + 1) * BLK]
                    p_one = both[BLK:, i * BLK : (i + 1) * BLK]
                    bias = bias_got[j % (nb // 2)][0:1]
                    p_one = p_one + jnp.where((row == BLK - 1) & (f == nf // 2 - 1), bias, 0.0)
                    p_zero = p_zero + jnp.where((row == 0) & (f == nf // 2), bias, 0.0)
                    carried = j * BLK + lane < 64 * f
                    gw[j] = jnp.where(carried, p_one, p_zero)
                    ext_ref[...] = ext_ref[...] + jnp.where(
                        j == m, p_one[BLK - 8 :, :], jnp.zeros((8, BLK), F32)
                    )

    round_c(0)
    round_c(1)
    round_e(0)
    round_a(1)
    round_c(2)
    round_e(1)
    full_left()
    round_x1(0)
    round_a(2)
    round_c(3)
    round_e(2)
    bias_on()
    round_x1(1)
    round_x2(0)
    round_a(3)
    round_e(3)
    round_x1(2)
    round_x2(1)
    arrive(bias_got, r_by)
    gradient_quad(0)
    round_a(4)
    finish_sums()
    round_x1(3)
    round_x2(2)
    gradient_quad(1)
    round_x1(4)
    round_x2(3)
    gradient_quad(2)
    write_cotangents()
    round_x2(4)
    gradient_quad(3)
    gradient_quad(4)

    @pl.loop(0, nb)
    def _(b):
        first = gw[(b + m) % nb]
        second = gw[(b + m + 1) % nb]
        mixed = pltpu.roll(jnp.where(low, second, first), 64, 1)
        g2[pl.ds(b, BLK, stride=nb), :] = jnp.where(par == 1, mixed, first)

    one_scale = 1.0 / fixes[0]
    two_scale = 1.0 / fixes[1]

    def adam(grad, param, mom_one, mom_two):
        new_one = beta_one * mom_one + (1.0 - beta_one) * grad
        new_two = beta_two * mom_two + (1.0 - beta_two) * grad * grad
        direction = (new_one * one_scale) / (jnp.sqrt(new_two * two_scale) + adam_eps)
        return new_one, new_two, param - learn_rate * (direction + decay_rate * param)

    loads[1].wait()
    loads[2].wait()
    rows_each = 4
    span = rows_each * nb

    def adam_rows(i):
        at = pl.ds(pl.multiple_of(i * span, span), span)
        flat = pl.ds(pl.multiple_of(i * span * BLK, span * BLK), span * BLK)
        new_one, new_two, updated = adam(
            g2[at, :], p2[at, :], m1[flat].reshape(span, BLK), m2[flat].reshape(span, BLK)
        )
        o1[at, :] = new_one
        o2[at, :] = new_two
        p2[at, :] = updated
        return (updated * updated).reshape(rows_each, nb, BLK)

    acc_ref[...] = jnp.zeros((nb, BLK), F32)
    steps = BLK // rows_each

    @pl.loop(0, steps - 1)
    def _(i):
        acc_ref[...] = acc_ref[...] + jnp.sum(adam_rows(i), axis=0)

    squares = adam_rows(steps - 1)
    acc_main = acc_ref[...] + jnp.sum(squares[: rows_each - 1], axis=0)
    acc_last = squares[rows_each - 1]
    ext_row = ext_ref[...]
    ext_row = jnp.where(par == 1, pltpu.roll(ext_row, 64, 1), ext_row)[7:8]
    ext_one, ext_two, ext_up = adam(
        ext_row, tails[pl.ds(0, 1), :], tails[pl.ds(1, 1), :], tails[pl.ds(2, 1), :]
    )
    o1[pl.ds(nb * BLK, 8), :] = jnp.broadcast_to(ext_one, (8, BLK))
    o2[pl.ds(nb * BLK, 8), :] = jnp.broadcast_to(ext_two, (8, BLK))
    writes = [
        pltpu.make_async_copy(o1, n1_out, out_sem.at[0]),
        pltpu.make_async_copy(o2, n2_out, out_sem.at[1]),
    ]
    for write in writes:
        write.start()

    lane_row = lax.broadcasted_iota(jnp.int32, (1, BLK), 1)
    heads = lax.broadcasted_iota(jnp.int32, (nb, BLK), 1)
    blocks = lax.broadcasted_iota(jnp.int32, (nb, BLK), 0)
    low_b = heads < 64
    ext_sq = jnp.sum(jnp.where(lane_row < 64, ext_up * ext_up, 0.0), axis=1, keepdims=True)

    def head_of(part):
        spot = f + 2 * blocks + part
        carry = spot // nf
        by_column = (spot % nf) // 2
        main = jnp.where(h == 0, f, by_column)
        last_q = jnp.where(f + carry < nf // 2, f + carry, by_column)
        return main, last_q

    ext_head = jnp.where(f + 1 < nf // 2, f + 1, f // 2)
    total = jnp.where(lane_row == ext_head, ext_sq, 0.0)
    maps = [head_of(0), head_of(1)]
    for part in range(2):
        inside = low_b if part == 0 else jnp.logical_not(low_b)
        for which, acc in enumerate((acc_main, acc_last)):
            sums = jnp.sum(jnp.where(inside, acc, 0.0), axis=1, keepdims=True)
            total = total + jnp.sum(
                jnp.where(maps[part][which] == heads, sums, 0.0), axis=0, keepdims=True
            )
    s_own[...] = jnp.broadcast_to(total, (8, BLK))
    me = z * CORES + c
    s_grp[me] = s_own[...]
    for i, (dz, dc) in enumerate(group):
        zz, cc = zw(z + dz), (c + dc) % CORES
        send_later(s_own, s_grp.at[me], s_sg.at[i], r_sg.at[me], x, fid(y, zz, cc))
    for dz, dc in group:
        other = zw(z + dz) * CORES + (c + dc) % CORES
        arrive(s_grp.at[other], r_sg.at[other])
    s_mid[...] = jnp.sum(s_grp[...], axis=0)
    s_col[y] = s_mid[...]
    for dy in range(1, NY):
        yy = (y + dy) % NY
        send_later(s_mid, s_col.at[y], s_ss.at[dy - 1], r_ss.at[y], x, fid(yy, z, c))
    for dy in range(1, NY):
        yy = (y + dy) % NY
        arrive(s_col.at[yy], r_ss.at[yy])
    sumsq = jnp.sum(s_col[...], axis=0)[0:1]
    threshold = learn_rate * lasso_weight * math.sqrt(2 * HD * dim + HD)
    shrink = jnp.maximum(1.0 - threshold / jnp.sqrt(sumsq + norm_eps), 0.0)

    def factor(which):
        sides = [
            jnp.sum(jnp.where(maps[part][which] == heads, shrink, 0.0), axis=1, keepdims=True)
            for part in range(2)
        ]
        return jnp.where(low_b, sides[0], sides[1])

    acc_ref[...] = factor(0)
    last_ref[...] = factor(1)
    ext_shrink = jnp.sum(jnp.where(lane_row == ext_head, shrink, 0.0), axis=1, keepdims=True)

    @pl.loop(0, steps - 1)
    def _(i):
        at = pl.ds(pl.multiple_of(i * span, span), span)
        block = p2[at, :].reshape(rows_each, nb, BLK) * acc_ref[...][None]
        p2[at, :] = block.reshape(span, BLK)

    end = (steps - 1) * span
    at = pl.ds(end, span - nb)
    block = p2[at, :].reshape(rows_each - 1, nb, BLK) * acc_ref[...][None]
    p2[at, :] = block.reshape(span - nb, BLK)
    at = pl.ds(end + span - nb, nb)
    p2[at, :] = p2[at, :] * last_ref[...]
    p2[pl.ds(nb * BLK, 8), :] = jnp.broadcast_to(ext_up * ext_shrink, (8, BLK))
    final = pltpu.make_async_copy(p2, np_out, out_sem.at[2])
    final.start()

    for copy in pending:
        copy.wait_send()
    for i in range(half_y):
        for cc in range(CORES):
            yd = half_y * c + i

            @pl.when((yd != y) | (cc != c))
            def _(i=i, cc=cc, yd=yd):
                for src, ss in ((xblk, s_ry), (pb.at[z, i], s_sy)):
                    pltpu.make_async_remote_copy(
                        src_ref=src, dst_ref=src, send_sem=ss.at[i, cc], recv_sem=r_sw,
                        device_id=(x, partner), device_id_type=MESH,
                    ).wait_send()

    def sent(src, ss):
        pltpu.make_async_remote_copy(
            src_ref=src, dst_ref=src, send_sem=ss, recv_sem=r_sw,
            device_id=(x, partner), device_id_type=MESH,
        ).wait_send()

    @pl.when(left_dst != f)
    def _():
        sent(lsend, s_lf.at[0])

    @pl.when(gives_row)
    def _():
        sent(lsend.at[pl.ds(pl.multiple_of(c * (BLK - 16), 16), 16)], s_lf.at[1])

    for write in writes:
        write.wait()
    final.wait()


def on_device(
    nz, hidden, grad_query, attn_out, grad_output, flat_params, moment_one, moment_two, step_count
):
    nb = NY * nz
    cells = nb * BLK * BLK
    rows = nb * BLK
    shard_len = flat_params.shape[0]
    step_num = step_count[0].astype(F32)
    fixes = jnp.stack(
        [
            1.0 - jnp.power(jnp.float32(beta_one), step_num),
            1.0 - jnp.power(jnp.float32(beta_two), step_num),
        ]
    )
    tails = jnp.stack([flat_params[cells:], moment_one[cells:], moment_two[cells:]])
    tails = jnp.pad(tails, ((0, 5), (0, BLK - 64)))
    vm = lambda shape, dtype=F32: pltpu.VMEM(shape, dtype)
    dma = lambda *shape: pltpu.SemaphoreType.DMA(shape) if shape else pltpu.SemaphoreType.DMA
    grp = nz * CORES
    whole = pl.BlockSpec(memory_space=pltpu.VMEM)
    anywhere = pl.BlockSpec(memory_space=pl.ANY)
    scratch = [
        vm((cells,)), vm((cells,)), vm((cells,)),
        vm((rows + 8, BLK)), vm((rows + 8, BLK)), vm((rows + 8, BLK)), vm((rows, BLK)),
        vm((nb, BLK, BLK)),
        vm((TOK, BLK), BF16), vm((TOK, BLK), BF16), vm((TOK, BLK), BF16), vm((BLK, TOK), BF16),
        vm((NX, BLK, TOK), BF16), vm((NX, 16, TOK), BF16),
        vm((BLK + 32, TOK)), vm((2 * BLK, NX * TOK), BF16), vm((TOK, 2 * BLK), BF16),
        vm((NX, nz, NY, TOK, BLK), BF16),
        vm((nz, NY // 2, TOK, BLK)), vm((nz, NY // 2, TOK, BLK)), vm((nz, NY // 2, TOK, BLK)),
        vm((nz, NY // 2, TOK, BLK)), vm((NY, TOK, BLK)),
        vm((8, BLK)), vm((grp, 8, BLK)), vm((grp, 8, BLK)),
        vm((8, BLK)), vm((nb, BLK)), vm((nb, BLK)),
        vm((8, BLK)), vm((grp, 8, BLK)), vm((8, BLK)), vm((NY, 8, BLK)),
        dma(3), dma(3), dma(), dma(), dma(NY // 2, CORES), dma(NY), dma(2), dma(2),
        dma(NX - 1, 2), dma(NX, 2),
        dma(grp - 1), dma(grp), dma(), dma(), dma(nz), dma(nz), dma(nz, 2), dma(nz, 2),
        dma(nz, 2), dma(nz, 2), dma(NX, nz), dma(NX, nz),
        dma(nz), dma(nz), dma(nz), dma(nz), dma(NY // 2, CORES), dma(NY),
        dma(grp - 1), dma(grp), dma(NY - 1), dma(NY),
    ]
    outs = pl.pallas_call(
        functools.partial(kernel, nz),
        out_shape=[
            jax.ShapeDtypeStruct((TOK, 64), BF16),
            jax.ShapeDtypeStruct((TOK, 64), BF16),
            jax.ShapeDtypeStruct((rows + 8, BLK), F32),
            jax.ShapeDtypeStruct((rows + 8, BLK), F32),
            jax.ShapeDtypeStruct((rows + 8, BLK), F32),
        ],
        in_specs=[whole] * 5 + [pl.BlockSpec(memory_space=pltpu.SMEM)] + [anywhere] * 3,
        out_specs=[whole] * 2 + [anywhere] * 3,
        scratch_shapes=scratch,
        compiler_params=pltpu.CompilerParams(
            collective_id=0, has_side_effects=True, vmem_limit_bytes=48 * 1024 * 1024
        ),
        cost_estimate=pl.CostEstimate(
            flops=4 * 512 * 128 * 4096, bytes_accessed=6 * 2 * 1024 * 1024, transcendentals=524352
        ),
        name="step",
    )(
        hidden, grad_query, attn_out, grad_output, tails, fixes,
        flat_params, moment_one, moment_two,
    )
    grad_hidden, grad_attn = outs[:2]
    new_params, new_one, new_two = (part.reshape(-1)[:shard_len] for part in outs[2:])
    return (grad_hidden, grad_attn, new_params, new_one, new_two)


def solution(mesh):
    nz = mesh.shape["fsdp"] // (NY * CORES)
    in_specs = (
        P("dp", "fsdp"),
        P("dp", "fsdp"),
        P("dp", "fsdp"),
        P("dp", "fsdp"),
        P("fsdp"),
        P("fsdp"),
        P("fsdp"),
        P(),
    )
    out_specs = (P("dp", "fsdp"), P("dp", "fsdp"), P("fsdp"), P("fsdp"), P("fsdp"))
    return jax.shard_map(
        functools.partial(on_device, nz), mesh=mesh, in_specs=in_specs, out_specs=out_specs, check_vma=False
    )
```

time: 630 us -> 82.8 us (0.13)
  waiting for transfers between devices: 353 us -> 0 us
  blocking collectives: 152 us -> 0 us
  Pallas kernels: 0 us -> 66.5 us
  local copies, waits for them, and re-layouts: 76.1 us -> 14.3 us
  other arithmetic: 21.8 us -> 0.09 us
  between operations: 15.1 us -> 1.39 us
  matrix products: 6.47 us -> 0 us
    all_gather x6 -> x0, waiting for transfers between devices: 350 us -> none  [the longest x1 81.4 us: on_device(): lax.all_gather(attn_out, 'fsdp', axis=1, tiled=True)]
    psum x2 -> x0, blocking collectives: 140 us -> none  [the longest x1 126 us: on_device(): sumsq = lax.psum(from_rows + from_cols, 'fsdp')]
    pallas_call x0 -> x1, Pallas kernels: none -> 66.5 us  [on_device(): pl.pallas_call(functools.partial(kernel, nz), out_shape=[jax.ShapeDtypeSt...]
    dynamic_update_slice x2 -> x0, local copies, waits for them, and re-layouts: 36.2 us -> none  [window_of(): buffer = lax.dynamic_update_slice(buffer, values, (lead_cells,))]
    concatenate x1 -> x0, local copies, waits for them, and re-layouts: 13.1 us -> none  [left_window(): joined = jnp.concatenate([query_all, gap_col, output_all, padding], axis=1)]
    all_gather x1 -> x0, blocking collectives: 11.7 us -> none  [on_device(): lax.all_gather(own_left, 'dp', axis=0, tiled=True)]
    mul x2 -> x0, other arithmetic: 8.46 us -> none  [the longest x1 5.99 us: on_device(): squares = updated_win * updated_win]
    dot_general x3 -> x0, matrix products: 6.47 us -> none  [the longest x1 5.4 us: only_query(): lax.dot_general(left_win, hidden_all, contract, preferred_element_type=jn...]
  transfers between devices with their start and end apart: 7 -> 0, of which waited for: 6 -> 0; matrix products, arithmetic and copies ran while one was open for 15% -> 0% of each run, Pallas kernels for 0% -> 0%
where the time goes in v1:
time: 82.8 us; the launch traced here: 82.2 us
  Pallas kernels  66.5 us (80%)
  local copies, waits for them, and re-layouts  14.3 us (17%)
  between operations  1.39 us (2%)
    pallas_call x1, Pallas kernels, on_device(): pl.pallas_call(functools.partial(kernel, nz), out_shape=[jax.ShapeDtypeSt...  66.5 us
    unnamed x13, local copies, waits for them, and re-layouts  12.9 us

profile of v1, /device:TPU:1, one launch (start us, length us, event | category | flops | bytes accessed | tf_op | source)
XLA Modules:
  0.0 82.2 jit_solution(15457726396593299524)
XLA Ops:
  1.4 0.1 pad_maximum_fusion.fixes
  1.4 0.7 slice_bitcast_fusion.2
  2.1 0.7 slice_bitcast_fusion
  2.8 0.8 %copy.13.hb = bf16[128,64]{1,0:T(8,128)(2,1)S(1)} copy(bf16[128,64]{0,1:T(8,128)(2,1)} %param.8) | data formatting | bytes 32768 | tf_op args[0]
  3.7 0.8 %copy.14.gb = bf16[128,64]{1,0:T(8,128)(2,1)S(1)} copy(bf16[128,64]{0,1:T(8,128)(2,1)} %param.9) | data formatting | bytes 32768 | tf_op args[1]
  4.5 0.8 %copy.15.ab = bf16[128,64]{1,0:T(8,128)(2,1)S(1)} copy(bf16[128,64]{0,1:T(8,128)(2,1)} %param.10) | data formatting | bytes 32768 | tf_op args[2]
  5.3 0.8 %copy.16.ob = bf16[128,64]{1,0:T(8,128)(2,1)S(1)} copy(bf16[128,64]{0,1:T(8,128)(2,1)} %param.11) | data formatting | bytes 32768 | tf_op args[3]
  6.2 66.5 %step.1 = (bf16[128,64]{1,0:T(8,128)(2,1)S(1)}, bf16[128,64]{1,0:T(8,128)(2,1)S(1)}, f32[4104,128]{1,0:T(8,128)S(1)}, f32[4104,128]{1,0:T(8,128)S(1)}, f32[4104,128]{1,0:T(8,128)}) custom-call(bf16[128,64]{1,0:T(8,128)(2,1)S(1)} %copy.13.hb, bf16[128,64]{1,0:T(8,128)(2,1)S(1)} %copy.14.gb, bf16[128,64]{1,0:T(8,128)(2,1)S(1)} %copy.15.ab, ...), custom_call_target="tpu_custom_call" | custom-call | flops 1073741824 | bytes 12582912 | tf_op jit(solution)/shard_map/step/pallas_call | solution.py:662
  72.6 0.0 copy-start
  72.7 1.3 %copy-done = f32[4104,128]{1,0:T(8,128)} copy-done((f32[4104,128]{1,0:T(8,128)}, f32[4104,128]{1,0:T(8,128)S(1)}, u32[]{:S(2)}) %copy-start) | copy-done | bytes 2101272
  74.0 0.7 copy.17
  74.7 0.7 copy.18
  75.4 3.0 %copy.23 = f32[524352]{0:T(1024)} copy(f32[524352]{0:T(1024)} %bitcast.13) | data formatting | bytes 4194816
  78.4 0.0 copy-start.1
  78.4 1.5 %copy.24 = f32[524352]{0:T(1024)} copy(f32[524352]{0:T(1024)S(1)} %bitcast.12) | data formatting | bytes 4194816
  79.9 0.9 %copy-done.1 = f32[4104,128]{1,0:T(8,128)S(1)} copy-done((f32[4104,128]{1,0:T(8,128)S(1)}, f32[4104,128]{1,0:T(8,128)}, u32[]{:S(2)}) %copy-start.1) | copy-done | bytes 2101272
  80.8 1.5 %copy.25 = f32[524352]{0:T(1024)} copy(f32[524352]{0:T(1024)S(1)} %bitcast.14) | data formatting | bytes 4194816
  (1 shorter events, 0.0 us)
Async XLA Ops:
  72.6 1.3 %copy-start = (f32[4104,128]{1,0:T(8,128)}, f32[4104,128]{1,0:T(8,128)S(1)}, u32[]{:S(2)}) copy-start(f32[4104,128]{1,0:T(8,128)S(1)} %get-tuple-element.12) | copy-start | bytes 6303748
  78.4 2.4 %copy-start.1 = (f32[4104,128]{1,0:T(8,128)S(1)}, f32[4104,128]{1,0:T(8,128)}, u32[]{:S(2)}) copy-start(f32[4104,128]{1,0:T(8,128)} %get-tuple-element.14) | copy-start | bytes 6303748

commit v2 on v1

--- a/solution.py
+++ b/solution.py
@@ -30,16 +30,17 @@
 
 
 def kernel(
-    nz, hb, gb, ab, ob, tails, fixes, p_hbm, m1_hbm, m2_hbm,
-    gh_out, ga_out, np_out, n1_out, n2_out,
+    nz, acts, p_tail, m1_tail, m2_tail, fixes, p_hbm, m1_hbm, m2_hbm,
+    gh_out, ga_out, up_out, n1_out, n2_out, factor_out,
     p1, m1, m2, p2, o1, o2, g2, gw,
-    pack, rpack, xblk, lsend, lb, rg, lt, ll, lown,
+    lb, rg, lt, ll, lown,
     rbuf, pb, xs, xr, ring, yb, bias_own, bias_grp, bias_got,
-    ext_ref, acc_ref, last_ref, s_own, s_grp, s_mid, s_col,
-    in_sem, out_sem, s_sw, r_sw, s_ry, r_ry, s_lf, r_lf, s_lx, r_lx,
+    ext_ref, acc_ref, s_own, s_grp,
+    in_sem, out_sem, self_sem, s_ry, r_ry, s_lf, r_lf, s_lx, r_lx,
     s_bg, r_bg, s_by, r_by, s_rz, r_rz, s_r1, r_r1, s_r2, r_r2, s_rp, r_rp,
-    s_sp, r_sp, s_sr, r_sr, s_sy, r_sy, s_sg, r_sg, s_ss, r_ss,
+    s_sp, r_sp, s_sr, r_sr, s_sy, r_sy, s_sg, r_sg,
 ):
+    h_in, gq_in, a_in, go_in = (acts.at[i] for i in range(4))
     nf = NY * nz * CORES
     nb = NY * nz
     dim = nb * BLK
@@ -84,7 +85,7 @@
 
     def arrive(dst, rs):
         pltpu.make_async_remote_copy(
-            src_ref=dst, dst_ref=dst, send_sem=s_sw, recv_sem=rs,
+            src_ref=dst, dst_ref=dst, send_sem=s_by, recv_sem=rs,
             device_id=(x, partner), device_id_type=MESH,
         ).wait_recv()
 
@@ -110,79 +111,69 @@
     for dx in range(1, NX):
         greet((x + dx) % NX, f)
     fl = f % (nf // 2)
-    left_src = 2 * fl + h
     row_src = 2 * (fl + 1 - 2 * h) + h
     row_chip = fl + 1 - 2 * h
     has_row = (row_chip >= 0) & (row_chip < nf // 2)
-    left_dst = c * (nf // 2) + k
+    left_dsts = (k, nf // 2 + k)
+    left_srcs = (2 * fl, 2 * fl + 1)
     row_dst_low = k - 1 + 2 * c
     gives_row = (row_dst_low >= 0) & (row_dst_low < nf // 2)
     row_dst = c * (nf // 2) + row_dst_low
 
-    @pl.when(left_src != f)
-    def _():
-        greet(x, left_src)
+    for src in left_srcs:
+
+        @pl.when(src != f)
+        def _(src=src):
+            greet(x, src)
 
     @pl.when(has_row)
     def _():
         greet(x, row_src)
 
-    own_pack = jnp.where(
-        c == 0,
-        jnp.concatenate([hb[...], gb[...]], axis=1).astype(F32),
-        jnp.concatenate([ab[...], ob[...]], axis=1).astype(F32),
-    )
-    pack[...] = jnp.where(
-        c == 0,
-        jnp.concatenate([ab[...], ob[...]], axis=1).astype(F32),
-        jnp.concatenate([hb[...], gb[...]], axis=1).astype(F32),
-    ).astype(BF16)
-
     greeted = len(group) + (NY - 1) * CORES + NX - 1
-    greeted = greeted + (left_dst != f).astype(jnp.int32) + gives_row.astype(jnp.int32)
+    for dst in left_dsts:
+        greeted = greeted + (dst != f).astype(jnp.int32)
+    greeted = greeted + gives_row.astype(jnp.int32)
     pl.semaphore_wait(barrier, greeted)
 
-    send_later(pack, rpack, s_sw, r_sw, x, partner)
     lane = lax.broadcasted_iota(jnp.int32, (BLK, BLK), 1)
     row = lax.broadcasted_iota(jnp.int32, (BLK, BLK), 0)
     low = lane < 64
-    arrive(rpack, r_sw)
-    got = rpack[...].astype(F32)
-    even = jnp.where(c == 0, own_pack, got)
-    odd = jnp.where(c == 0, got, own_pack)
-    right = jnp.where(low, even, pltpu.roll(odd, 64, 1))
-    left = jnp.where(low, pltpu.roll(even, 64, 1), odd)
-    xblk[...] = right.astype(BF16)
-
-    for i in range(half_y):
-        for cc in range(CORES):
-            yd = half_y * c + i
-
-            @pl.when((yd != y) | (cc != c))
-            def _(i=i, cc=cc, yd=yd):
-                send(xblk, rbuf.at[x, z, y], s_ry.at[i, cc], r_ry.at[y], x, fid(yd, z, cc))
-
-    @pl.when(h == c)
-    def _():
-        rbuf[x, z, y] = right.astype(BF16)
-
-    left_t = jnp.transpose(left)
-    lsend[...] = left_t.astype(BF16)
-
-    @pl.when(left_dst != f)
-    def _():
-        send(lsend, lb.at[x], s_lf.at[0], r_lf.at[0], x, left_dst)
-
-    @pl.when(left_dst == f)
-    def _():
-        lb[x] = left_t.astype(BF16)
-
-    @pl.when(gives_row)
-    def _():
-        send(
-            lsend.at[pl.ds(pl.multiple_of(c * (BLK - 16), 16), 16)],
-            rg.at[x], s_lf.at[1], r_lf.at[1], x, row_dst,
-        )
+    own_half = pl.ds(pl.multiple_of(c * 64, 64), 64)
+
+    def right_sends():
+        for yd in range(NY):
+            src = h_in if yd < half_y else a_in
+            for cc in range(CORES):
+                yield yd, cc, src
+
+    for yd, cc, src in right_sends():
+        remote = (yd != y) | (cc != c)
+
+        @pl.when(remote)
+        def _(yd=yd, cc=cc, src=src):
+            send(
+                src, rbuf.at[x, z, y, own_half], s_ry.at[yd, cc], r_ry.at[y, c], x, fid(yd, z, cc)
+            )
+
+        @pl.when(jnp.logical_not(remote))
+        def _(src=src):
+            pltpu.make_async_copy(src, rbuf.at[x, z, y, own_half], self_sem.at[0]).start()
+
+    row_part = lambda src: src.at[pl.ds(pl.multiple_of(c * (64 - 16), 16), 16)]
+    for i, (src, dst) in enumerate(zip((gq_in, go_in), left_dsts)):
+
+        @pl.when(dst != f)
+        def _(i=i, src=src, dst=dst):
+            send(src, lb.at[x, own_half], s_lf.at[i], r_lf.at[c], x, dst)
+
+        @pl.when(dst == f)
+        def _(src=src):
+            pltpu.make_async_copy(src, lb.at[x, own_half], self_sem.at[1]).start()
+
+        @pl.when(gives_row & (c == i))
+        def _(src=src):
+            send(row_part(src), rg.at[x], s_lf.at[2], r_lf.at[2], x, row_dst)
 
     @pl.when(jnp.logical_not(has_row))
     def _():
@@ -196,11 +187,17 @@
         p2[pl.ds(i * 8 * nb, 8 * nb), :] = p1[pl.ds(i * step_cells, step_cells)].reshape(8 * nb, BLK)
 
     pair = lambda cc: pl.ds(half_y * cc, half_y)
-    for yy in range(NY):
-
-        @pl.when((yy != y) | (h != c))
-        def _(yy=yy):
-            arrive(rbuf.at[x, z, yy], r_ry.at[yy])
+    def own_quad():
+        for yy in range(NY):
+            for cc in range(CORES):
+                remote = (yy != y) | (cc != c)
+                half = rbuf.at[x, z, yy, pl.ds(cc * 64, 64)]
+
+                @pl.when(remote)
+                def _(yy=yy, cc=cc, half=half):
+                    arrive(half, r_ry.at[yy, cc])
+
+        pltpu.make_async_copy(h_in, rbuf.at[x, z, y, own_half], self_sem.at[0]).wait()
 
     def z_quad(r):
         out = []
@@ -244,15 +241,22 @@
             ref = rbuf.at[x_far, zq, pair(c)]
             send_later(ref, ref, s_rp.at[x_far, zq], r_rp.at[x_far, zq], x, partner)
 
+    own_quad()
     round_a(0)
 
-    @pl.when(left_src != f)
-    def _():
-        arrive(lb.at[x], r_lf.at[0])
+    for cc, src in enumerate(left_srcs):
+
+        @pl.when(src != f)
+        def _(cc=cc):
+            arrive(lb.at[x, pl.ds(cc * 64, 64)], r_lf.at[cc])
+
+        @pl.when(src == f)
+        def _():
+            pltpu.make_async_copy(gq_in, lb.at[x, own_half], self_sem.at[1]).wait()
 
     @pl.when(has_row)
     def _():
-        arrive(rg.at[x], r_lf.at[1])
+        arrive(rg.at[x], r_lf.at[2])
 
     for dx in range(1, NX):
         xx = (x + dx) % NX
@@ -274,8 +278,15 @@
     lown[:, pl.ds(0, BLK)] = jnp.transpose(zero).astype(BF16)
     lown[:, pl.ds(BLK, BLK)] = jnp.transpose(one).astype(BF16)
 
-    tail_p = tails[pl.ds(0, 1), :]
-    tail_here = jnp.where(par == 1, pltpu.roll(tails[...], 64, 1)[0:1], tail_p)
+    lane_row = lax.broadcasted_iota(jnp.int32, (1, BLK), 1)
+
+    def tail_row(ref):
+        return jnp.where(lane_row < 64, ref[...].reshape(8, BLK)[0:1], 0.0)
+
+    tail_p = tail_row(p_tail)
+    tail_here = jnp.where(
+        par == 1, pltpu.roll(jnp.broadcast_to(tail_p, (8, BLK)), 64, 1)[0:1], tail_p
+    )
 
     def window_block(j):
         first = p2[pl.ds((j - m + nb) % nb, BLK, stride=nb), :]
@@ -361,8 +372,8 @@
             total = yb[base_y]
             for i in range(1, half_y):
                 total = total + yb[base_y + i]
-            total = jnp.where(c == 1, pltpu.roll(total, 64, 1), total)
-            out[...] = total[:, :64].astype(BF16)
+            total = jnp.transpose(total)
+            out[...] = jnp.where(c == 1, total[64:], total[:64]).astype(BF16)
 
     def full_left():
         for xx in range(NX):
@@ -405,12 +416,12 @@
             for yy in range(0, NY, 2):
                 wide = jnp.concatenate(
                     [
-                        jnp.concatenate([rbuf[xx, zq, yy], rbuf[xx, zq, yy + 1]], axis=1)
+                        jnp.concatenate([rbuf[xx, zq, yy], rbuf[xx, zq, yy + 1]], axis=0)
                         for xx in range(NX)
                     ],
-                    axis=0,
+                    axis=1,
                 )
-                both = jnp.dot(ll[...], wide, preferred_element_type=F32)
+                both = lax.dot_general(ll[...], wide, NT, preferred_element_type=F32)
                 for i in range(2):
                     j = (yy + i) * nz + zq
                     p_zero = both[:BLK, i * BLK : (i + 1) * BLK]
@@ -424,45 +435,50 @@
                         j == m, p_one[BLK - 8 :, :], jnp.zeros((8, BLK), F32)
                     )
 
+    def reorder(zc):
+        for yy in range(NY):
+            j = yy * nz + zc
+            first = gw[j]
+            second = gw[(j + 1) % nb]
+            mixed = pltpu.roll(jnp.where(low, second, first), 64, 1)
+            g2[pl.ds((j - m + nb) % nb, BLK, stride=nb), :] = jnp.where(par == 1, mixed, first)
+
+    def gradient(r):
+        gradient_quad(r)
+        if 0 < r <= longs:
+            reorder(zw(z - r))
+            reorder(zw(z + r - 1))
+
     round_c(0)
     round_c(1)
+    round_a(1)
     round_e(0)
-    round_a(1)
     round_c(2)
-    round_e(1)
+    round_x1(0)
     full_left()
-    round_x1(0)
     round_a(2)
     round_c(3)
-    round_e(2)
-    bias_on()
     round_x1(1)
     round_x2(0)
+    round_e(1)
+    bias_on()
     round_a(3)
-    round_e(3)
     round_x1(2)
     round_x2(1)
-    arrive(bias_got, r_by)
-    gradient_quad(0)
+    round_e(2)
     round_a(4)
-    finish_sums()
     round_x1(3)
     round_x2(2)
-    gradient_quad(1)
+    arrive(bias_got, r_by)
+    gradient(0)
+    round_e(3)
     round_x1(4)
     round_x2(3)
-    gradient_quad(2)
-    write_cotangents()
+    gradient(1)
+    gradient(2)
     round_x2(4)
-    gradient_quad(3)
-    gradient_quad(4)
-
-    @pl.loop(0, nb)
-    def _(b):
-        first = gw[(b + m) % nb]
-        second = gw[(b + m + 1) % nb]
-        mixed = pltpu.roll(jnp.where(low, second, first), 64, 1)
-        g2[pl.ds(b, BLK, stride=nb), :] = jnp.where(par == 1, mixed, first)
+    gradient(3)
+    gradient(4)
 
     one_scale = 1.0 / fixes[0]
     two_scale = 1.0 / fixes[1]
@@ -502,18 +518,19 @@
     ext_row = ext_ref[...]
     ext_row = jnp.where(par == 1, pltpu.roll(ext_row, 64, 1), ext_row)[7:8]
     ext_one, ext_two, ext_up = adam(
-        ext_row, tails[pl.ds(0, 1), :], tails[pl.ds(1, 1), :], tails[pl.ds(2, 1), :]
+        ext_row, tail_p, tail_row(m1_tail), tail_row(m2_tail)
     )
     o1[pl.ds(nb * BLK, 8), :] = jnp.broadcast_to(ext_one, (8, BLK))
     o2[pl.ds(nb * BLK, 8), :] = jnp.broadcast_to(ext_two, (8, BLK))
+    p2[pl.ds(nb * BLK, 8), :] = jnp.broadcast_to(ext_up, (8, BLK))
     writes = [
+        pltpu.make_async_copy(p2, up_out, out_sem.at[2]),
         pltpu.make_async_copy(o1, n1_out, out_sem.at[0]),
         pltpu.make_async_copy(o2, n2_out, out_sem.at[1]),
     ]
     for write in writes:
         write.start()
 
-    lane_row = lax.broadcasted_iota(jnp.int32, (1, BLK), 1)
     heads = lax.broadcasted_iota(jnp.int32, (nb, BLK), 1)
     blocks = lax.broadcasted_iota(jnp.int32, (nb, BLK), 0)
     low_b = heads < 64
@@ -537,24 +554,21 @@
             total = total + jnp.sum(
                 jnp.where(maps[part][which] == heads, sums, 0.0), axis=0, keepdims=True
             )
-    s_own[...] = jnp.broadcast_to(total, (8, BLK))
-    me = z * CORES + c
-    s_grp[me] = s_own[...]
-    for i, (dz, dc) in enumerate(group):
-        zz, cc = zw(z + dz), (c + dc) % CORES
-        send_later(s_own, s_grp.at[me], s_sg.at[i], r_sg.at[me], x, fid(y, zz, cc))
-    for dz, dc in group:
-        other = zw(z + dz) * CORES + (c + dc) % CORES
-        arrive(s_grp.at[other], r_sg.at[other])
-    s_mid[...] = jnp.sum(s_grp[...], axis=0)
-    s_col[y] = s_mid[...]
-    for dy in range(1, NY):
-        yy = (y + dy) % NY
-        send_later(s_mid, s_col.at[y], s_ss.at[dy - 1], r_ss.at[y], x, fid(yy, z, c))
-    for dy in range(1, NY):
-        yy = (y + dy) % NY
-        arrive(s_col.at[yy], r_ss.at[yy])
-    sumsq = jnp.sum(s_col[...], axis=0)[0:1]
+    s_own[...] = total
+    offsets = [
+        (dy, dz, dc)
+        for dy in range(NY)
+        for dz in range(nz)
+        for dc in range(CORES)
+        if (dy, dz, dc) != (0, 0, 0)
+    ]
+    offsets.sort(key=lambda o: -(min(o[0], NY - o[0]) + min(o[1], nz - o[1])))
+    for i, (dy, dz, dc) in enumerate(offsets):
+        target = fid((y + dy) % NY, zw(z + dz), (c + dc) % CORES)
+        send(s_own, s_grp.at[i], s_sg, r_sg, x, target)
+    finish_sums()
+    arrive(s_grp, r_sg)
+    sumsq = s_own[...] + jnp.sum(s_grp[...], axis=0)
     threshold = learn_rate * lasso_weight * math.sqrt(2 * HD * dim + HD)
     shrink = jnp.maximum(1.0 - threshold / jnp.sqrt(sumsq + norm_eps), 0.0)
 
@@ -565,57 +579,89 @@
         ]
         return jnp.where(low_b, sides[0], sides[1])
 
-    acc_ref[...] = factor(0)
-    last_ref[...] = factor(1)
+    factor_out[pl.ds(0, nb), :] = factor(0)
+    factor_out[pl.ds(nb, nb), :] = factor(1)
     ext_shrink = jnp.sum(jnp.where(lane_row == ext_head, shrink, 0.0), axis=1, keepdims=True)
-
-    @pl.loop(0, steps - 1)
-    def _(i):
-        at = pl.ds(pl.multiple_of(i * span, span), span)
-        block = p2[at, :].reshape(rows_each, nb, BLK) * acc_ref[...][None]
-        p2[at, :] = block.reshape(span, BLK)
-
-    end = (steps - 1) * span
-    at = pl.ds(end, span - nb)
-    block = p2[at, :].reshape(rows_each - 1, nb, BLK) * acc_ref[...][None]
-    p2[at, :] = block.reshape(span - nb, BLK)
-    at = pl.ds(end + span - nb, nb)
-    p2[at, :] = p2[at, :] * last_ref[...]
-    p2[pl.ds(nb * BLK, 8), :] = jnp.broadcast_to(ext_up * ext_shrink, (8, BLK))
-    final = pltpu.make_async_copy(p2, np_out, out_sem.at[2])
-    final.start()
-
+    factor_out[pl.ds(2 * nb, 8), :] = jnp.broadcast_to(ext_shrink, (8, BLK))
+
+    write_cotangents()
+
+    def sent(src, ss):
+        pltpu.make_async_remote_copy(
+            src_ref=src, dst_ref=src, send_sem=ss, recv_sem=r_by,
+            device_id=(x, partner), device_id_type=MESH,
+        ).wait_send()
+
+    sent(s_grp, s_sg)
     for copy in pending:
         copy.wait_send()
+    for yd, cc, src in right_sends():
+
+        @pl.when((yd != y) | (cc != c))
+        def _(yd=yd, cc=cc, src=src):
+            sent(src, s_ry.at[yd, cc])
+
     for i in range(half_y):
         for cc in range(CORES):
             yd = half_y * c + i
 
             @pl.when((yd != y) | (cc != c))
-            def _(i=i, cc=cc, yd=yd):
-                for src, ss in ((xblk, s_ry), (pb.at[z, i], s_sy)):
-                    pltpu.make_async_remote_copy(
-                        src_ref=src, dst_ref=src, send_sem=ss.at[i, cc], recv_sem=r_sw,
-                        device_id=(x, partner), device_id_type=MESH,
-                    ).wait_send()
-
-    def sent(src, ss):
-        pltpu.make_async_remote_copy(
-            src_ref=src, dst_ref=src, send_sem=ss, recv_sem=r_sw,
-            device_id=(x, partner), device_id_type=MESH,
-        ).wait_send()
-
-    @pl.when(left_dst != f)
-    def _():
-        sent(lsend, s_lf.at[0])
+            def _(i=i, cc=cc):
+                sent(pb.at[z, i], s_sy.at[i, cc])
+
+    for i, (src, dst) in enumerate(zip((gq_in, go_in), left_dsts)):
+
+        @pl.when(dst != f)
+        def _(i=i, src=src):
+            sent(src, s_lf.at[i])
 
     @pl.when(gives_row)
     def _():
-        sent(lsend.at[pl.ds(pl.multiple_of(c * (BLK - 16), 16), 16)], s_lf.at[1])
+        sent(row_part(gq_in), s_lf.at[2])
 
     for write in writes:
         write.wait()
-    final.wait()
+
+
+def finish(nb, gh, ga, up, n1, n2, factors, gh_out, ga_out, np_out, n1_out, n2_out, scaled, sems):
+    copies = [
+        pltpu.make_async_copy(gh, gh_out, sems.at[6]),
+        pltpu.make_async_copy(ga, ga_out, sems.at[7]),
+        pltpu.make_async_copy(n1, n1_out, sems.at[0]),
+        pltpu.make_async_copy(n2, n2_out, sems.at[1]),
+    ]
+    for copy in copies:
+        copy.start()
+    pieces, rows_each = 4, 4
+    span = rows_each * nb
+    steps = BLK // rows_each // pieces
+    main = factors[pl.ds(0, nb), :]
+    for piece in range(pieces):
+        start = piece * steps * span
+        full = steps - 1 if piece == pieces - 1 else steps
+
+        @pl.loop(0, full)
+        def _(i):
+            at = pl.ds(pl.multiple_of(start + i * span, span), span)
+            block = up[at, :].reshape(rows_each, nb, BLK) * factors[pl.ds(0, nb), :][None]
+            scaled[at, :] = block.reshape(span, BLK)
+
+        rows = steps * span
+        if piece == pieces - 1:
+            at = pl.ds(start + full * span, span - nb)
+            block = up[at, :].reshape(rows_each - 1, nb, BLK) * main[None]
+            scaled[at, :] = block.reshape(span - nb, BLK)
+            at = pl.ds(nb * BLK - nb, nb)
+            scaled[at, :] = up[at, :] * factors[pl.ds(nb, nb), :]
+            at = pl.ds(nb * BLK, 8)
+            scaled[at, :] = up[at, :] * factors[pl.ds(2 * nb, 8), :]
+            rows += 8
+        at = pl.ds(start, rows)
+        copy = pltpu.make_async_copy(scaled.at[at], np_out.at[at], sems.at[2 + piece])
+        copy.start()
+        copies.append(copy)
+    for copy in copies:
+        copy.wait()
 
 
 def on_device(
@@ -632,8 +678,6 @@
             1.0 - jnp.power(jnp.float32(beta_two), step_num),
         ]
     )
-    tails = jnp.stack([flat_params[cells:], moment_one[cells:], moment_two[cells:]])
-    tails = jnp.pad(tails, ((0, 5), (0, BLK - 64)))
     vm = lambda shape, dtype=F32: pltpu.VMEM(shape, dtype)
     dma = lambda *shape: pltpu.SemaphoreType.DMA(shape) if shape else pltpu.SemaphoreType.DMA
     grp = nz * CORES
@@ -643,47 +687,57 @@
         vm((cells,)), vm((cells,)), vm((cells,)),
         vm((rows + 8, BLK)), vm((rows + 8, BLK)), vm((rows + 8, BLK)), vm((rows, BLK)),
         vm((nb, BLK, BLK)),
-        vm((TOK, BLK), BF16), vm((TOK, BLK), BF16), vm((TOK, BLK), BF16), vm((BLK, TOK), BF16),
         vm((NX, BLK, TOK), BF16), vm((NX, 16, TOK), BF16),
         vm((BLK + 32, TOK)), vm((2 * BLK, NX * TOK), BF16), vm((TOK, 2 * BLK), BF16),
         vm((NX, nz, NY, TOK, BLK), BF16),
         vm((nz, NY // 2, TOK, BLK)), vm((nz, NY // 2, TOK, BLK)), vm((nz, NY // 2, TOK, BLK)),
         vm((nz, NY // 2, TOK, BLK)), vm((NY, TOK, BLK)),
         vm((8, BLK)), vm((grp, 8, BLK)), vm((grp, 8, BLK)),
-        vm((8, BLK)), vm((nb, BLK)), vm((nb, BLK)),
-        vm((8, BLK)), vm((grp, 8, BLK)), vm((8, BLK)), vm((NY, 8, BLK)),
-        dma(3), dma(3), dma(), dma(), dma(NY // 2, CORES), dma(NY), dma(2), dma(2),
+        vm((8, BLK)), vm((nb, BLK)),
+        vm((1, BLK)), vm((NY * grp - 1, 1, BLK)),
+        dma(3), dma(3), dma(2), dma(NY, CORES), dma(NY, CORES), dma(3), dma(3),
         dma(NX - 1, 2), dma(NX, 2),
         dma(grp - 1), dma(grp), dma(), dma(), dma(nz), dma(nz), dma(nz, 2), dma(nz, 2),
         dma(nz, 2), dma(nz, 2), dma(NX, nz), dma(NX, nz),
         dma(nz), dma(nz), dma(nz), dma(nz), dma(NY // 2, CORES), dma(NY),
-        dma(grp - 1), dma(grp), dma(NY - 1), dma(NY),
+        dma(), dma(),
     ]
+    cotangent = jax.ShapeDtypeStruct((64, TOK), BF16)
+    flat = jax.ShapeDtypeStruct((rows + 8, BLK), F32)
+    tail = pl.BlockSpec((1024,), lambda i: (cells // 1024,))
     outs = pl.pallas_call(
         functools.partial(kernel, nz),
+        grid=(1,),
         out_shape=[
-            jax.ShapeDtypeStruct((TOK, 64), BF16),
-            jax.ShapeDtypeStruct((TOK, 64), BF16),
-            jax.ShapeDtypeStruct((rows + 8, BLK), F32),
-            jax.ShapeDtypeStruct((rows + 8, BLK), F32),
-            jax.ShapeDtypeStruct((rows + 8, BLK), F32),
+            cotangent, cotangent,
+            flat, flat, flat,
+            jax.ShapeDtypeStruct((2 * nb + 8, BLK), F32),
         ],
-        in_specs=[whole] * 5 + [pl.BlockSpec(memory_space=pltpu.SMEM)] + [anywhere] * 3,
-        out_specs=[whole] * 2 + [anywhere] * 3,
+        in_specs=[anywhere] + [tail] * 3 + [pl.BlockSpec(memory_space=pltpu.SMEM)] + [anywhere] * 3,
+        out_specs=[whole] * 2 + [anywhere] * 3 + [whole],
         scratch_shapes=scratch,
         compiler_params=pltpu.CompilerParams(
-            collective_id=0, has_side_effects=True, vmem_limit_bytes=48 * 1024 * 1024
+            collective_id=0, has_side_effects=True, vmem_limit_bytes=46 * 1024 * 1024
         ),
         cost_estimate=pl.CostEstimate(
             flops=4 * 512 * 128 * 4096, bytes_accessed=6 * 2 * 1024 * 1024, transcendentals=524352
         ),
         name="step",
     )(
-        hidden, grad_query, attn_out, grad_output, tails, fixes,
-        flat_params, moment_one, moment_two,
+        jnp.stack([hidden.T, grad_query.T, attn_out.T, grad_output.T]),
+        flat_params, moment_one, moment_two, fixes, flat_params, moment_one, moment_two,
     )
-    grad_hidden, grad_attn = outs[:2]
-    new_params, new_one, new_two = (part.reshape(-1)[:shard_len] for part in outs[2:])
+    results = pl.pallas_call(
+        functools.partial(finish, nb),
+        out_shape=[cotangent] * 2 + [flat] * 3,
+        in_specs=[anywhere, anywhere, whole, anywhere, anywhere, whole],
+        out_specs=[anywhere] * 5,
+        scratch_shapes=[vm((rows + 8, BLK)), dma(8)],
+        compiler_params=pltpu.CompilerParams(vmem_limit_bytes=16 * 1024 * 1024),
+        name="finish",
+    )(*outs)
+    grad_hidden, grad_attn = results[0].T, results[1].T
+    new_params, new_one, new_two = (part.reshape(-1)[:shard_len] for part in results[2:])
     return (grad_hidden, grad_attn, new_params, new_one, new_two)
 
 

time: 82.8 us -> 62.4 us (0.75)
  local copies, waits for them, and re-layouts: 14.3 us -> 0 us
  Pallas kernels: 66.5 us -> 59.9 us
    unnamed x13 -> x0, local copies, waits for them, and re-layouts: 12.9 us -> none
    pallas_call x1 -> x2, Pallas kernels: 66.5 us -> 59.9 us  [the longest x1 57.2 us: on_device(): pl.pallas_call(functools.partial(kernel, nz), grid=(1,), out_shape=[cotan...]
    another operation x2 -> x0, local copies, waits for them, and re-layouts: 1.39 us -> none  [on_device(): jnp.stack([flat_params[cells:], moment_one[cells:], moment_two[cells:]])]
where the time goes in v2:
time: 62.4 us; the launch traced here: 62.1 us
  Pallas kernels  59.9 us (96%)
  between operations  1.37 us (2%)
  other arithmetic  0.86 us (1%)
    pallas_call x1, Pallas kernels, on_device(): pl.pallas_call(functools.partial(kernel, nz), grid=(1,), out_shape=[cotan...  57.2 us
    pallas_call x1, Pallas kernels, on_device(): pl.pallas_call(functools.partial(finish, nb), out_shape=[cotangent] * 2 +...  2.74 us

profile of v2, /device:TPU:1, one launch (start us, length us, event | category | flops | bytes accessed | tf_op | source)
XLA Modules:
  0.0 62.1 jit_solution(10898169095578944980)
XLA Ops:
  1.4 0.1 pad_maximum_fusion.1.fixes
  1.4 0.8 %pad_maximum_fusion.acts = bf16[4,64,128]{2,1,0:T(8,128)(2,1)S(1)} fusion(bf16[1,64,128]{2,1,0:T(8,128)(2,1)} %bitcast.20, bf16[1,64,128]{2,1,0:T(8,128)(2,1)} %bitcast.21, bf16[1,64,128]{2,1,0:T(8,128)(2,1)} %bitcast.22, bf16[1,64,128]{2,1,0:T(8,128)(2,1)} %bitcast.23), kind=kLoop, calls=%fused_computation | loop fusion | flops 98304 | bytes 131072 | tf_op jit(solution)/shard_map/stack | solution.py:727
  2.2 57.2 %step.1 = (bf16[64,128]{1,0:T(8,128)(2,1)S(1)}, bf16[64,128]{1,0:T(8,128)(2,1)S(1)}, f32[4104,128]{1,0:T(8,128)S(1)}, f32[4104,128]{1,0:T(8,128)S(1)}, f32[4104,128]{1,0:T(8,128)S(1)}, /*index=5*/f32[72,128]{1,0:T(8,128)S(1)}) custom-call(bf16[4,64,128]{2,1,0:T(8,128)(2,1)S(1)} %pad_maximum_fusion.acts, f32[524352]{0:T(1024)} %p_hbm.1, f32[524352]{0:T(1024)} %m1_hbm.1, ...), custom_call_target="tpu_custom_call" | custom-call | flops 1073741824 | bytes 12582912 | tf_op jit(solution)/shard_map/step/pallas_call | solution.py:708
  59.4 2.7 %finish.1 = (bf16[64,128]{1,0:T(8,128)(2,1)}, bf16[64,128]{1,0:T(8,128)(2,1)}, f32[4104,128]{1,0:T(8,128)}, f32[4104,128]{1,0:T(8,128)}, f32[4104,128]{1,0:T(8,128)}) custom-call(bf16[64,128]{1,0:T(8,128)(2,1)S(1)} %get-tuple-element.16.gh, bf16[64,128]{1,0:T(8,128)(2,1)S(1)} %get-tuple-element.17.ga, f32[4104,128]{1,0:T(8,128)S(1)} %get-tuple-element.18.up, ...), custom_call_target="tpu_custom_call" | custom-call | tf_op jit(solution)/shard_map/finish/pallas_call | solution.py:730

commit v3 on v2

--- a/solution.py
+++ b/solution.py
@@ -32,9 +32,9 @@
 def kernel(
     nz, acts, p_tail, m1_tail, m2_tail, fixes, p_hbm, m1_hbm, m2_hbm,
     gh_out, ga_out, up_out, n1_out, n2_out, factor_out,
-    p1, m1, m2, p2, o1, o2, g2, gw,
+    p1, m1, m2, p2, o1, o2, pw, gb, gw,
     lb, rg, lt, ll, lown,
-    rbuf, pb, xs, xr, ring, yb, bias_own, bias_grp, bias_got,
+    wins, rbuf, pb, xs, xr, ring, yb, bias_own, bias_grp, bias_got,
     ext_ref, acc_ref, s_own, s_grp,
     in_sem, out_sem, self_sem, s_ry, r_ry, s_lf, r_lf, s_lx, r_lx,
     s_bg, r_bg, s_by, r_by, s_rz, r_rz, s_r1, r_r1, s_r2, r_r2, s_rp, r_rp,
@@ -134,11 +134,12 @@
     for dst in left_dsts:
         greeted = greeted + (dst != f).astype(jnp.int32)
     greeted = greeted + gives_row.astype(jnp.int32)
-    pl.semaphore_wait(barrier, greeted)
-
     lane = lax.broadcasted_iota(jnp.int32, (BLK, BLK), 1)
     row = lax.broadcasted_iota(jnp.int32, (BLK, BLK), 0)
     low = lane < 64
+
+    pl.semaphore_wait(barrier, greeted)
+
     own_half = pl.ds(pl.multiple_of(c * 64, 64), 64)
 
     def right_sends():
@@ -180,11 +181,12 @@
         rg[x] = jnp.zeros((16, TOK), BF16)
 
     loads[0].wait()
-    step_cells = 8 * dim
+    group_cells = 8 * dim
 
     @pl.loop(0, BLK // 8)
     def _(i):
-        p2[pl.ds(i * 8 * nb, 8 * nb), :] = p1[pl.ds(i * step_cells, step_cells)].reshape(8 * nb, BLK)
+        some = p1[pl.ds(i * group_cells, group_cells)].reshape(8, nb, BLK)
+        pw[:, pl.ds(pl.multiple_of(i * 8, 8), 8), :] = jnp.swapaxes(some, 0, 1)
 
     pair = lambda cc: pl.ds(half_y * cc, half_y)
     def own_quad():
@@ -244,6 +246,35 @@
     own_quad()
     round_a(0)
 
+    lane_row = lax.broadcasted_iota(jnp.int32, (1, BLK), 1)
+
+    def tail_row(ref):
+        return jnp.where(lane_row < 64, ref[...].reshape(8, BLK)[0:1], 0.0)
+
+    tail_p = tail_row(p_tail)
+    tail_here = jnp.where(
+        par == 1, pltpu.roll(jnp.broadcast_to(tail_p, (8, BLK)), 64, 1)[0:1], tail_p
+    )
+
+    def window_block(j):
+        first = pw[(j - m + nb) % nb]
+        second = pw[(j - m - 1 + nb) % nb]
+        mixed = pltpu.roll(jnp.where(low, first, second), 64, 1)
+        block = jnp.where(par == 1, mixed, first)
+        column = j * BLK + lane
+        carried = column < 64 * f
+        top = jnp.where(carried, 0.0, block)
+        bottom = jnp.where(carried, block, 0.0)
+        is_tail = (row == BLK - 1) & (column >= 64 * f) & (column < 64 * f + 64)
+        bottom = jnp.where(is_tail, tail_here, bottom)
+        return jnp.concatenate([top, bottom], axis=0).astype(BF16)
+
+    @pl.loop(0, nz)
+    def _(d):
+        for hh in range(2):
+            for i in range(half_y):
+                wins[d, hh, :, i * BLK : (i + 1) * BLK] = window_block((half_y * hh + i) * nz + d)
+
     for cc, src in enumerate(left_srcs):
 
         @pl.when(src != f)
@@ -278,36 +309,10 @@
     lown[:, pl.ds(0, BLK)] = jnp.transpose(zero).astype(BF16)
     lown[:, pl.ds(BLK, BLK)] = jnp.transpose(one).astype(BF16)
 
-    lane_row = lax.broadcasted_iota(jnp.int32, (1, BLK), 1)
-
-    def tail_row(ref):
-        return jnp.where(lane_row < 64, ref[...].reshape(8, BLK)[0:1], 0.0)
-
-    tail_p = tail_row(p_tail)
-    tail_here = jnp.where(
-        par == 1, pltpu.roll(jnp.broadcast_to(tail_p, (8, BLK)), 64, 1)[0:1], tail_p
-    )
-
-    def window_block(j):
-        first = p2[pl.ds((j - m + nb) % nb, BLK, stride=nb), :]
-        second = p2[pl.ds((j - m - 1 + nb) % nb, BLK, stride=nb), :]
-        mixed = pltpu.roll(jnp.where(low, first, second), 64, 1)
-        block = jnp.where(par == 1, mixed, first)
-        column = j * BLK + lane
-        carried = column < 64 * f
-        top = jnp.where(carried, 0.0, block)
-        bottom = jnp.where(carried, block, 0.0)
-        is_tail = (row == BLK - 1) & (column >= 64 * f) & (column < 64 * f + 64)
-        bottom = jnp.where(is_tail, tail_here, bottom)
-        return jnp.concatenate([top, bottom], axis=0).astype(BF16)
-
     def partial_chunk(d):
         for mine in range(2):
             hh = c if mine == 0 else 1 - c
-            wide = jnp.concatenate(
-                [window_block((half_y * hh + i) * nz + d) for i in range(half_y)], axis=1
-            )
-            part = jnp.dot(lown[...], wide, preferred_element_type=F32)
+            part = jnp.dot(lown[...], wins[d, hh], preferred_element_type=F32)
             for i in range(half_y):
                 target = pb if mine == 0 else xs
                 target[d, i] = part[:, i * BLK : (i + 1) * BLK]
@@ -390,15 +395,16 @@
             jnp.ones((8, NX * TOK), BF16), ll[pl.ds(0, BLK), :], NT, preferred_element_type=F32
         )
         me = z * CORES + c
-        bias_grp[me] = bias_own[...]
+        bias_grp[pl.ds(pl.multiple_of(me * 8, 8), 8), :] = bias_own[...]
         for i, (dz, dc) in enumerate(group):
             zz, cc = zw(z + dz), (c + dc) % CORES
-            send_later(bias_own, bias_grp.at[me], s_bg.at[i], r_bg.at[me], x, fid(y, zz, cc))
+            mine = bias_grp.at[pl.ds(pl.multiple_of(me * 8, 8), 8)]
+            send_later(bias_own, mine, s_bg.at[i], r_bg.at[me], x, fid(y, zz, cc))
 
     def bias_on():
         for dz, dc in group:
             other = zw(z + dz) * CORES + (c + dc) % CORES
-            arrive(bias_grp.at[other], r_bg.at[other])
+            arrive(bias_grp.at[pl.ds(pl.multiple_of(other * 8, 8), 8)], r_bg.at[other])
         send_later(bias_grp, bias_got, s_by, r_by, x, fid((y + 1) % NY, z, c))
 
     ext_ref[...] = jnp.zeros((8, BLK), F32)
@@ -426,9 +432,6 @@
                     j = (yy + i) * nz + zq
                     p_zero = both[:BLK, i * BLK : (i + 1) * BLK]
                     p_one = both[BLK:, i * BLK : (i + 1) * BLK]
-                    bias = bias_got[j % (nb // 2)][0:1]
-                    p_one = p_one + jnp.where((row == BLK - 1) & (f == nf // 2 - 1), bias, 0.0)
-                    p_zero = p_zero + jnp.where((row == 0) & (f == nf // 2), bias, 0.0)
                     carried = j * BLK + lane < 64 * f
                     gw[j] = jnp.where(carried, p_one, p_zero)
                     ext_ref[...] = ext_ref[...] + jnp.where(
@@ -441,7 +444,7 @@
             first = gw[j]
             second = gw[(j + 1) % nb]
             mixed = pltpu.roll(jnp.where(low, second, first), 64, 1)
-            g2[pl.ds((j - m + nb) % nb, BLK, stride=nb), :] = jnp.where(par == 1, mixed, first)
+            gb[(j - m + nb) % nb] = jnp.where(par == 1, mixed, first)
 
     def gradient(r):
         gradient_quad(r)
@@ -449,36 +452,54 @@
             reorder(zw(z - r))
             reorder(zw(z + r - 1))
 
+    def bias_rows():
+        arrive(bias_got, r_by)
+        half = nb // 2
+        sums = bias_got[pl.ds(0, half, stride=8), :]
+        turned = pltpu.roll(sums, 64, 1)
+        index = lax.broadcasted_iota(jnp.int32, (half, BLK), 0)
+        before = jnp.where(index == 0, 0.0, pltpu.roll(turned, 1, 0))
+        left_half = lax.broadcasted_iota(jnp.int32, (half, BLK), 1) < 64
+        nothing = jnp.zeros((half, BLK), F32)
+        last = jnp.where(left_half, before, turned)
+        here_first = f == nf // 2
+        here_last = f == nf // 2 - 1
+        ext_ref[...] = ext_ref[...] + jnp.where(here_last, sums[half - 1 : half], 0.0)
+        return (
+            jnp.where(here_first, jnp.concatenate([sums, nothing], axis=0), 0.0),
+            jnp.where(here_last, jnp.concatenate([nothing, last], axis=0), 0.0),
+        )
+
     round_c(0)
     round_c(1)
     round_a(1)
     round_e(0)
+    round_x1(0)
     round_c(2)
-    round_x1(0)
-    full_left()
     round_a(2)
-    round_c(3)
     round_x1(1)
     round_x2(0)
+    round_c(3)
+    full_left()
+    round_a(3)
     round_e(1)
-    bias_on()
-    round_a(3)
     round_x1(2)
     round_x2(1)
+    gradient(0)
+    round_a(4)
     round_e(2)
-    round_a(4)
     round_x1(3)
     round_x2(2)
-    arrive(bias_got, r_by)
-    gradient(0)
-    round_e(3)
+    bias_on()
+    gradient(1)
     round_x1(4)
     round_x2(3)
-    gradient(1)
+    round_e(3)
     gradient(2)
     round_x2(4)
     gradient(3)
     gradient(4)
+    bias_first, bias_last = bias_rows()
 
     one_scale = 1.0 / fixes[0]
     two_scale = 1.0 / fixes[1]
@@ -491,28 +512,37 @@
 
     loads[1].wait()
     loads[2].wait()
-    rows_each = 4
+    rows_each = 8
     span = rows_each * nb
-
-    def adam_rows(i):
+    steps = BLK // rows_each
+
+    def adam_rows(i, bias_top=None, bias_bottom=None):
         at = pl.ds(pl.multiple_of(i * span, span), span)
         flat = pl.ds(pl.multiple_of(i * span * BLK, span * BLK), span * BLK)
+        grad = gb[:, pl.ds(pl.multiple_of(i * rows_each, rows_each), rows_each), :]
+        grad = jnp.swapaxes(grad, 0, 1)
+        if bias_top is not None:
+            grad = jnp.concatenate([grad[:1] + bias_top[None], grad[1:]], axis=0)
+        if bias_bottom is not None:
+            grad = jnp.concatenate([grad[:-1], grad[-1:] + bias_bottom[None]], axis=0)
         new_one, new_two, updated = adam(
-            g2[at, :], p2[at, :], m1[flat].reshape(span, BLK), m2[flat].reshape(span, BLK)
+            grad.reshape(span, BLK),
+            p1[flat].reshape(span, BLK),
+            m1[flat].reshape(span, BLK),
+            m2[flat].reshape(span, BLK),
         )
         o1[at, :] = new_one
         o2[at, :] = new_two
         p2[at, :] = updated
         return (updated * updated).reshape(rows_each, nb, BLK)
 
-    acc_ref[...] = jnp.zeros((nb, BLK), F32)
-    steps = BLK // rows_each
-
-    @pl.loop(0, steps - 1)
+    acc_ref[...] = jnp.sum(adam_rows(0, bias_top=bias_first), axis=0)
+
+    @pl.loop(1, steps - 1)
     def _(i):
         acc_ref[...] = acc_ref[...] + jnp.sum(adam_rows(i), axis=0)
 
-    squares = adam_rows(steps - 1)
+    squares = adam_rows(steps - 1, bias_bottom=bias_last)
     acc_main = acc_ref[...] + jnp.sum(squares[: rows_each - 1], axis=0)
     acc_last = squares[rows_each - 1]
     ext_row = ext_ref[...]
@@ -685,14 +715,14 @@
     anywhere = pl.BlockSpec(memory_space=pl.ANY)
     scratch = [
         vm((cells,)), vm((cells,)), vm((cells,)),
-        vm((rows + 8, BLK)), vm((rows + 8, BLK)), vm((rows + 8, BLK)), vm((rows, BLK)),
-        vm((nb, BLK, BLK)),
+        vm((rows + 8, BLK)), vm((rows + 8, BLK)), vm((rows + 8, BLK)),
+        vm((nb, BLK, BLK)), vm((nb, BLK, BLK)), vm((nb, BLK, BLK)),
         vm((NX, BLK, TOK), BF16), vm((NX, 16, TOK), BF16),
         vm((BLK + 32, TOK)), vm((2 * BLK, NX * TOK), BF16), vm((TOK, 2 * BLK), BF16),
-        vm((NX, nz, NY, TOK, BLK), BF16),
+        vm((nz, 2, 2 * BLK, NY // 2 * BLK), BF16), vm((NX, nz, NY, TOK, BLK), BF16),
         vm((nz, NY // 2, TOK, BLK)), vm((nz, NY // 2, TOK, BLK)), vm((nz, NY // 2, TOK, BLK)),
         vm((nz, NY // 2, TOK, BLK)), vm((NY, TOK, BLK)),
-        vm((8, BLK)), vm((grp, 8, BLK)), vm((grp, 8, BLK)),
+        vm((8, BLK)), vm((grp * 8, BLK)), vm((grp * 8, BLK)),
         vm((8, BLK)), vm((nb, BLK)),
         vm((1, BLK)), vm((NY * grp - 1, 1, BLK)),
         dma(3), dma(3), dma(2), dma(NY, CORES), dma(NY, CORES), dma(3), dma(3),

time: 62.4 us -> 57.8 us (0.926)
  Pallas kernels: 59.9 us -> 55.3 us
    pallas_call x1, Pallas kernels: 57.2 us -> 52.6 us  [on_device(): pl.pallas_call(functools.partial(kernel, nz), grid=(1,), out_shape=[cotan...]
where the time goes in v3:
time: 57.8 us; the launch traced here: 57.5 us
  Pallas kernels  55.3 us (96%)
  between operations  1.37 us (2%)
  other arithmetic  0.86 us (1%)
    pallas_call x1, Pallas kernels, on_device(): pl.pallas_call(functools.partial(kernel, nz), grid=(1,), out_shape=[cotan...  52.6 us
    pallas_call x1, Pallas kernels, on_device(): pl.pallas_call(functools.partial(finish, nb), out_shape=[cotangent] * 2 +...  2.74 us

profile of v3, /device:TPU:1, one launch (start us, length us, event | category | flops | bytes accessed | tf_op | source)
XLA Modules:
  0.0 57.5 jit_solution(4739741790293048446)
XLA Ops:
  1.4 0.1 pad_maximum_fusion.1.fixes
  1.4 0.8 %pad_maximum_fusion.acts = bf16[4,64,128]{2,1,0:T(8,128)(2,1)S(1)} fusion(bf16[1,64,128]{2,1,0:T(8,128)(2,1)} %bitcast.20, bf16[1,64,128]{2,1,0:T(8,128)(2,1)} %bitcast.21, bf16[1,64,128]{2,1,0:T(8,128)(2,1)} %bitcast.22, bf16[1,64,128]{2,1,0:T(8,128)(2,1)} %bitcast.23), kind=kLoop, calls=%fused_computation | loop fusion | flops 98304 | bytes 131072 | tf_op jit(solution)/shard_map/stack | solution.py:757
  2.2 52.6 %step.1 = (bf16[64,128]{1,0:T(8,128)(2,1)S(1)}, bf16[64,128]{1,0:T(8,128)(2,1)S(1)}, f32[4104,128]{1,0:T(8,128)S(1)}, f32[4104,128]{1,0:T(8,128)S(1)}, f32[4104,128]{1,0:T(8,128)S(1)}, /*index=5*/f32[72,128]{1,0:T(8,128)S(1)}) custom-call(bf16[4,64,128]{2,1,0:T(8,128)(2,1)S(1)} %pad_maximum_fusion.acts, f32[524352]{0:T(1024)} %p_hbm.1, f32[524352]{0:T(1024)} %m1_hbm.1, ...), custom_call_target="tpu_custom_call" | custom-call | flops 1073741824 | bytes 12582912 | tf_op jit(solution)/shard_map/step/pallas_call | solution.py:738
  54.8 2.7 %finish.1 = (bf16[64,128]{1,0:T(8,128)(2,1)}, bf16[64,128]{1,0:T(8,128)(2,1)}, f32[4104,128]{1,0:T(8,128)}, f32[4104,128]{1,0:T(8,128)}, f32[4104,128]{1,0:T(8,128)}) custom-call(bf16[64,128]{1,0:T(8,128)(2,1)S(1)} %get-tuple-element.16.gh, bf16[64,128]{1,0:T(8,128)(2,1)S(1)} %get-tuple-element.17.ga, f32[4104,128]{1,0:T(8,128)S(1)} %get-tuple-element.18.up, ...), custom_call_target="tpu_custom_call" | custom-call | tf_op jit(solution)/shard_map/finish/pallas_call | solution.py:760

commit v4 on v3

--- a/solution.py
+++ b/solution.py
@@ -14,6 +14,7 @@
 CORES = 2
 TOK = 128
 BLK = 128
+DIRECT = 4
 
 beta_one = 0.9
 beta_two = 0.95
@@ -34,10 +35,10 @@
     gh_out, ga_out, up_out, n1_out, n2_out, factor_out,
     p1, m1, m2, p2, o1, o2, pw, gb, gw,
     lb, rg, lt, ll, lown,
-    wins, rbuf, pb, xs, xr, ring, yb, bias_own, bias_grp, bias_got,
+    wins, rbuf, pb, xs, xr, ring, yb, bias_own, bias_got, bias_add,
     ext_ref, acc_ref, s_own, s_grp,
     in_sem, out_sem, self_sem, s_ry, r_ry, s_lf, r_lf, s_lx, r_lx,
-    s_bg, r_bg, s_by, r_by, s_rz, r_rz, s_r1, r_r1, s_r2, r_r2, s_rp, r_rp,
+    s_by, r_by, s_rz, r_rz, s_r1, r_r1, s_r2, r_r2, s_rp, r_rp,
     s_sp, r_sp, s_sr, r_sr, s_sy, r_sy, s_sg, r_sg,
 ):
     h_in, gq_in, a_in, go_in = (acts.at[i] for i in range(4))
@@ -94,17 +95,16 @@
         pltpu.make_async_copy(src.at[pl.ds(0, cells)], dst, in_sem.at[i])
         for i, (src, dst) in enumerate(((p_hbm, p1), (m1_hbm, m1), (m2_hbm, m2)))
     ]
-    for load in loads:
-        load.start()
 
     barrier = pltpu.get_barrier_semaphore()
 
     def greet(xx, ff):
         pl.semaphore_signal(barrier, inc=1, device_id=(xx, ff), device_id_type=MESH)
 
-    group = [(dz, dc) for dz in range(nz) for dc in range(CORES) if (dz, dc) != (0, 0)]
-    for dz, dc in group:
-        greet(x, fid(y, zw(z + dz), (c + dc) % CORES))
+    near_z = sorted({1, nz - 1})
+    for dz in near_z:
+        greet(x, fid(y, zw(z + dz), c))
+    greet(x, partner)
     for dy in range(1, NY):
         for dc in range(CORES):
             greet(x, fid((y + dy) % NY, z, (c + dc) % CORES))
@@ -130,7 +130,7 @@
     def _():
         greet(x, row_src)
 
-    greeted = len(group) + (NY - 1) * CORES + NX - 1
+    greeted = len(near_z) + 1 + (NY - 1) * CORES + NX - 1
     for dst in left_dsts:
         greeted = greeted + (dst != f).astype(jnp.int32)
     greeted = greeted + gives_row.astype(jnp.int32)
@@ -179,6 +179,8 @@
     @pl.when(jnp.logical_not(has_row))
     def _():
         rg[x] = jnp.zeros((16, TOK), BF16)
+
+    loads[0].start()
 
     loads[0].wait()
     group_cells = 8 * dim
@@ -224,23 +226,31 @@
                 send_later(ref, ref, s_rz.at[2 * r + 2], r_rz.at[2 * r + 2], x, z_short)
             send_later(ref, ref, s_r1.at[idx, 0], r_r1.at[idx, 0], x_up, f)
             send_later(ref, ref, s_r1.at[idx, 1], r_r1.at[idx, 1], x_down, f)
+            if r >= DIRECT:
+                send_later(ref, ref, s_r2.at[idx, 0], r_r2.at[idx, 0], x_far, f)
             if r > 0:
                 send_later(ref, ref, s_rp.at[x, zq], r_rp.at[x, zq], x, partner)
 
     def round_x1(r):
         for idx, zq in z_quad(r):
-            for way, (frm, to) in enumerate(((x_down, x_up), (x_up, x_down))):
+            ways = ((x_down, x_up), (x_up, x_down))
+            for way, (frm, to) in enumerate(ways):
+                arrive(rbuf.at[frm, zq, pair(c)], r_r1.at[idx, way])
+                if r < DIRECT:
+                    part = rbuf.at[frm, zq, half_y * c + way]
+                    send_later(part, part, s_r2.at[idx, way], r_r2.at[idx, way], to, f)
+            for frm, _ in ways:
                 ref = rbuf.at[frm, zq, pair(c)]
-                arrive(ref, r_r1.at[idx, way])
-                part = rbuf.at[frm, zq, half_y * c + way]
-                send_later(part, part, s_r2.at[idx, way], r_r2.at[idx, way], to, f)
                 send_later(ref, ref, s_rp.at[frm, zq], r_rp.at[frm, zq], x, partner)
 
     def round_x2(r):
         for idx, zq in z_quad(r):
-            for way in range(2):
-                arrive(rbuf.at[x_far, zq, half_y * c + way], r_r2.at[idx, way])
             ref = rbuf.at[x_far, zq, pair(c)]
+            if r < DIRECT:
+                for way in range(2):
+                    arrive(rbuf.at[x_far, zq, half_y * c + way], r_r2.at[idx, way])
+            else:
+                arrive(ref, r_r2.at[idx, 0])
             send_later(ref, ref, s_rp.at[x_far, zq], r_rp.at[x_far, zq], x, partner)
 
     own_quad()
@@ -394,18 +404,15 @@
         bias_own[...] = lax.dot_general(
             jnp.ones((8, NX * TOK), BF16), ll[pl.ds(0, BLK), :], NT, preferred_element_type=F32
         )
-        me = z * CORES + c
-        bias_grp[pl.ds(pl.multiple_of(me * 8, 8), 8), :] = bias_own[...]
-        for i, (dz, dc) in enumerate(group):
-            zz, cc = zw(z + dz), (c + dc) % CORES
-            mine = bias_grp.at[pl.ds(pl.multiple_of(me * 8, 8), 8)]
-            send_later(bias_own, mine, s_bg.at[i], r_bg.at[me], x, fid(y, zz, cc))
+
+    quarter = nf // 4
+    bias_dst = nf // 2 - 1 + f // quarter
+    bias_slot = pl.ds(pl.multiple_of((f % quarter) * 8, 8), 8)
 
     def bias_on():
-        for dz, dc in group:
-            other = zw(z + dz) * CORES + (c + dc) % CORES
-            arrive(bias_grp.at[pl.ds(pl.multiple_of(other * 8, 8), 8)], r_bg.at[other])
-        send_later(bias_grp, bias_got, s_by, r_by, x, fid((y + 1) % NY, z, c))
+        @pl.when(f < nf // 2)
+        def _():
+            send(bias_own, bias_got.at[bias_slot], s_by, r_by, x, bias_dst)
 
     ext_ref[...] = jnp.zeros((8, BLK), F32)
 
@@ -452,23 +459,28 @@
             reorder(zw(z - r))
             reorder(zw(z + r - 1))
 
+    bias_add[...] = jnp.zeros((2, nb, BLK), F32)
+
     def bias_rows():
-        arrive(bias_got, r_by)
         half = nb // 2
-        sums = bias_got[pl.ds(0, half, stride=8), :]
-        turned = pltpu.roll(sums, 64, 1)
-        index = lax.broadcasted_iota(jnp.int32, (half, BLK), 0)
-        before = jnp.where(index == 0, 0.0, pltpu.roll(turned, 1, 0))
-        left_half = lax.broadcasted_iota(jnp.int32, (half, BLK), 1) < 64
-        nothing = jnp.zeros((half, BLK), F32)
-        last = jnp.where(left_half, before, turned)
-        here_first = f == nf // 2
-        here_last = f == nf // 2 - 1
-        ext_ref[...] = ext_ref[...] + jnp.where(here_last, sums[half - 1 : half], 0.0)
-        return (
-            jnp.where(here_first, jnp.concatenate([sums, nothing], axis=0), 0.0),
-            jnp.where(here_last, jnp.concatenate([nothing, last], axis=0), 0.0),
-        )
+
+        @pl.when((f == nf // 2) | (f == nf // 2 - 1))
+        def _():
+            arrive(bias_got, r_by)
+            sums = bias_got[pl.ds(0, half, stride=8), :]
+
+            @pl.when(f == nf // 2)
+            def _():
+                bias_add[0, pl.ds(0, half)] = sums
+
+            @pl.when(f == nf // 2 - 1)
+            def _():
+                turned = pltpu.roll(sums, 64, 1)
+                index = lax.broadcasted_iota(jnp.int32, (half, BLK), 0)
+                before = jnp.where(index == 0, 0.0, pltpu.roll(turned, 1, 0))
+                left_half = lax.broadcasted_iota(jnp.int32, (half, BLK), 1) < 64
+                bias_add[1, pl.ds(half, half)] = jnp.where(left_half, before, turned)
+                ext_ref[...] = ext_ref[...] + sums[half - 1 : half]
 
     round_c(0)
     round_c(1)
@@ -481,16 +493,18 @@
     round_x2(0)
     round_c(3)
     full_left()
+    loads[1].start()
+    loads[2].start()
     round_a(3)
     round_e(1)
     round_x1(2)
     round_x2(1)
     gradient(0)
     round_a(4)
+    bias_on()
     round_e(2)
     round_x1(3)
     round_x2(2)
-    bias_on()
     gradient(1)
     round_x1(4)
     round_x2(3)
@@ -499,7 +513,7 @@
     round_x2(4)
     gradient(3)
     gradient(4)
-    bias_first, bias_last = bias_rows()
+    bias_rows()
 
     one_scale = 1.0 / fixes[0]
     two_scale = 1.0 / fixes[1]
@@ -536,13 +550,13 @@
         p2[at, :] = updated
         return (updated * updated).reshape(rows_each, nb, BLK)
 
-    acc_ref[...] = jnp.sum(adam_rows(0, bias_top=bias_first), axis=0)
+    acc_ref[...] = jnp.sum(adam_rows(0, bias_top=bias_add[0]), axis=0)
 
     @pl.loop(1, steps - 1)
     def _(i):
         acc_ref[...] = acc_ref[...] + jnp.sum(adam_rows(i), axis=0)
 
-    squares = adam_rows(steps - 1, bias_bottom=bias_last)
+    squares = adam_rows(steps - 1, bias_bottom=bias_add[1])
     acc_main = acc_ref[...] + jnp.sum(squares[: rows_each - 1], axis=0)
     acc_last = squares[rows_each - 1]
     ext_row = ext_ref[...]
@@ -554,12 +568,9 @@
     o2[pl.ds(nb * BLK, 8), :] = jnp.broadcast_to(ext_two, (8, BLK))
     p2[pl.ds(nb * BLK, 8), :] = jnp.broadcast_to(ext_up, (8, BLK))
     writes = [
-        pltpu.make_async_copy(p2, up_out, out_sem.at[2]),
-        pltpu.make_async_copy(o1, n1_out, out_sem.at[0]),
-        pltpu.make_async_copy(o2, n2_out, out_sem.at[1]),
+        pltpu.make_async_copy(ref, out, out_sem.at[sem])
+        for ref, out, sem in ((o1, n1_out, 0), (o2, n2_out, 1), (p2, up_out, 2))
     ]
-    for write in writes:
-        write.start()
 
     heads = lax.broadcasted_iota(jnp.int32, (nb, BLK), 1)
     blocks = lax.broadcasted_iota(jnp.int32, (nb, BLK), 0)
@@ -597,6 +608,8 @@
         target = fid((y + dy) % NY, zw(z + dz), (c + dc) % CORES)
         send(s_own, s_grp.at[i], s_sg, r_sg, x, target)
     finish_sums()
+    for write in writes:
+        write.start()
     arrive(s_grp, r_sg)
     sumsq = s_own[...] + jnp.sum(s_grp[...], axis=0)
     threshold = learn_rate * lasso_weight * math.sqrt(2 * HD * dim + HD)
@@ -648,6 +661,10 @@
     @pl.when(gives_row)
     def _():
         sent(row_part(gq_in), s_lf.at[2])
+
+    @pl.when(f < nf // 2)
+    def _():
+        sent(bias_own, s_by)
 
     for write in writes:
         write.wait()
@@ -722,12 +739,12 @@
         vm((nz, 2, 2 * BLK, NY // 2 * BLK), BF16), vm((NX, nz, NY, TOK, BLK), BF16),
         vm((nz, NY // 2, TOK, BLK)), vm((nz, NY // 2, TOK, BLK)), vm((nz, NY // 2, TOK, BLK)),
         vm((nz, NY // 2, TOK, BLK)), vm((NY, TOK, BLK)),
-        vm((8, BLK)), vm((grp * 8, BLK)), vm((grp * 8, BLK)),
+        vm((8, BLK)), vm((grp * 8, BLK)), vm((2, nb, BLK)),
         vm((8, BLK)), vm((nb, BLK)),
         vm((1, BLK)), vm((NY * grp - 1, 1, BLK)),
         dma(3), dma(3), dma(2), dma(NY, CORES), dma(NY, CORES), dma(3), dma(3),
         dma(NX - 1, 2), dma(NX, 2),
-        dma(grp - 1), dma(grp), dma(), dma(), dma(nz), dma(nz), dma(nz, 2), dma(nz, 2),
+        dma(), dma(), dma(nz), dma(nz), dma(nz, 2), dma(nz, 2),
         dma(nz, 2), dma(nz, 2), dma(NX, nz), dma(NX, nz),
         dma(nz), dma(nz), dma(nz), dma(nz), dma(NY // 2, CORES), dma(NY),
         dma(), dma(),

time: 57.8 us -> 56.8 us (0.983)
  Pallas kernels: 55.3 us -> 54.4 us
    pallas_call x1, Pallas kernels: 52.6 us -> 51.6 us  [on_device(): pl.pallas_call(functools.partial(kernel, nz), grid=(1,), out_shape=[cotan...]
where the time goes in v4:
time: 56.8 us; the launch traced here: 56.6 us
  Pallas kernels  54.4 us (96%)
  between operations  1.37 us (2%)
  other arithmetic  0.86 us (2%)
    pallas_call x1, Pallas kernels, on_device(): pl.pallas_call(functools.partial(kernel, nz), grid=(1,), out_shape=[cotan...  51.6 us
    pallas_call x1, Pallas kernels, on_device(): pl.pallas_call(functools.partial(finish, nb), out_shape=[cotangent] * 2 +...  2.74 us

profile of v4, /device:TPU:1, one launch (start us, length us, event | category | flops | bytes accessed | tf_op | source)
XLA Modules:
  0.0 56.6 jit_solution(9255714149559217296)
XLA Ops:
  1.4 0.1 pad_maximum_fusion.1.fixes
  1.4 0.8 %pad_maximum_fusion.acts = bf16[4,64,128]{2,1,0:T(8,128)(2,1)S(1)} fusion(bf16[1,64,128]{2,1,0:T(8,128)(2,1)} %bitcast.20, bf16[1,64,128]{2,1,0:T(8,128)(2,1)} %bitcast.21, bf16[1,64,128]{2,1,0:T(8,128)(2,1)} %bitcast.22, bf16[1,64,128]{2,1,0:T(8,128)(2,1)} %bitcast.23), kind=kLoop, calls=%fused_computation | loop fusion | flops 98304 | bytes 131072 | tf_op jit(solution)/shard_map/stack | solution.py:774
  2.2 51.6 %step.1 = (bf16[64,128]{1,0:T(8,128)(2,1)S(1)}, bf16[64,128]{1,0:T(8,128)(2,1)S(1)}, f32[4104,128]{1,0:T(8,128)S(1)}, f32[4104,128]{1,0:T(8,128)S(1)}, f32[4104,128]{1,0:T(8,128)S(1)}, /*index=5*/f32[72,128]{1,0:T(8,128)S(1)}) custom-call(bf16[4,64,128]{2,1,0:T(8,128)(2,1)S(1)} %pad_maximum_fusion.acts, f32[524352]{0:T(1024)} %p_hbm.1, f32[524352]{0:T(1024)} %m1_hbm.1, ...), custom_call_target="tpu_custom_call" | custom-call | flops 1073741824 | bytes 12582912 | tf_op jit(solution)/shard_map/step/pallas_call | solution.py:755
  53.9 2.7 %finish.1 = (bf16[64,128]{1,0:T(8,128)(2,1)}, bf16[64,128]{1,0:T(8,128)(2,1)}, f32[4104,128]{1,0:T(8,128)}, f32[4104,128]{1,0:T(8,128)}, f32[4104,128]{1,0:T(8,128)}) custom-call(bf16[64,128]{1,0:T(8,128)(2,1)S(1)} %get-tuple-element.16.gh, bf16[64,128]{1,0:T(8,128)(2,1)S(1)} %get-tuple-element.17.ga, f32[4104,128]{1,0:T(8,128)S(1)} %get-tuple-element.18.up, ...), custom_call_target="tpu_custom_call" | custom-call | tf_op jit(solution)/shard_map/finish/pallas_call | solution.py:777

commit v5 on v4

--- a/solution.py
+++ b/solution.py
@@ -33,7 +33,7 @@
 def kernel(
     nz, acts, p_tail, m1_tail, m2_tail, fixes, p_hbm, m1_hbm, m2_hbm,
     gh_out, ga_out, up_out, n1_out, n2_out, factor_out,
-    p1, m1, m2, p2, o1, o2, pw, gb, gw,
+    p1, m1, m2, p2, o1, o2, pw, m1w, m2w, gw, edge_in, gedge,
     lb, rg, lt, ll, lown,
     wins, rbuf, pb, xs, xr, ring, yb, bias_own, bias_got, bias_add,
     ext_ref, acc_ref, s_own, s_grp,
@@ -445,19 +445,59 @@
                         j == m, p_one[BLK - 8 :, :], jnp.zeros((8, BLK), F32)
                     )
 
-    def reorder(zc):
+    one_scale = 1.0 / fixes[0]
+    two_scale = 1.0 / fixes[1]
+
+    def adam(grad, param, mom_one, mom_two):
+        new_one = beta_one * mom_one + (1.0 - beta_one) * grad
+        new_two = beta_two * mom_two + (1.0 - beta_two) * grad * grad
+        direction = (new_one * one_scale) / (jnp.sqrt(new_two * two_scale) + adam_eps)
+        return new_one, new_two, param - learn_rate * (direction + decay_rate * param)
+
+    rows_each = 8
+    span = rows_each * nb
+
+    def by_block(source, target):
+        @pl.loop(0, BLK // rows_each)
+        def _(i):
+            flat = pl.ds(pl.multiple_of(i * span * BLK, span * BLK), span * BLK)
+            some = source[flat].reshape(rows_each, nb, BLK)
+            at = pl.ds(pl.multiple_of(i * rows_each, rows_each), rows_each)
+            target[:, at, :] = jnp.swapaxes(some, 0, 1)
+
+    def moments():
+        loads[1].wait()
+        loads[2].wait()
+        by_block(m1, m1w)
+        by_block(m2, m2w)
+        for n, ref in enumerate((pw, m1w, m2w)):
+            edge_in[n, 0] = jnp.swapaxes(ref[:, pl.ds(0, 8), :], 0, 1)[0]
+            edge_in[n, 1] = jnp.swapaxes(ref[:, pl.ds(BLK - 8, 8), :], 0, 1)[7]
+
+    inner = (row > 0) & (row < BLK - 1)
+
+    def adam_blocks(zc):
         for yy in range(NY):
             j = yy * nz + zc
             first = gw[j]
             second = gw[(j + 1) % nb]
             mixed = pltpu.roll(jnp.where(low, second, first), 64, 1)
-            gb[(j - m + nb) % nb] = jnp.where(par == 1, mixed, first)
+            grad = jnp.where(par == 1, mixed, first)
+            b = (j - m + nb) % nb
+            new_one, new_two, updated = adam(grad, pw[b], m1w[b], m2w[b])
+            m1w[b] = new_one
+            m2w[b] = new_two
+            pw[b] = updated
+            squares = jnp.where(inner, updated * updated, 0.0)
+            acc_ref[pl.ds(b, 1), :] = jnp.sum(squares, axis=0, keepdims=True)
+            gedge[0, pl.ds(b, 1), :] = grad[:1]
+            gedge[1, pl.ds(b, 1), :] = grad[BLK - 1 :]
 
     def gradient(r):
         gradient_quad(r)
         if 0 < r <= longs:
-            reorder(zw(z - r))
-            reorder(zw(z + r - 1))
+            adam_blocks(zw(z - r))
+            adam_blocks(zw(z + r - 1))
 
     bias_add[...] = jnp.zeros((2, nb, BLK), F32)
 
@@ -499,6 +539,7 @@
     round_e(1)
     round_x1(2)
     round_x2(1)
+    moments()
     gradient(0)
     round_a(4)
     bias_on()
@@ -515,50 +556,12 @@
     gradient(4)
     bias_rows()
 
-    one_scale = 1.0 / fixes[0]
-    two_scale = 1.0 / fixes[1]
-
-    def adam(grad, param, mom_one, mom_two):
-        new_one = beta_one * mom_one + (1.0 - beta_one) * grad
-        new_two = beta_two * mom_two + (1.0 - beta_two) * grad * grad
-        direction = (new_one * one_scale) / (jnp.sqrt(new_two * two_scale) + adam_eps)
-        return new_one, new_two, param - learn_rate * (direction + decay_rate * param)
-
-    loads[1].wait()
-    loads[2].wait()
-    rows_each = 8
-    span = rows_each * nb
-    steps = BLK // rows_each
-
-    def adam_rows(i, bias_top=None, bias_bottom=None):
-        at = pl.ds(pl.multiple_of(i * span, span), span)
-        flat = pl.ds(pl.multiple_of(i * span * BLK, span * BLK), span * BLK)
-        grad = gb[:, pl.ds(pl.multiple_of(i * rows_each, rows_each), rows_each), :]
-        grad = jnp.swapaxes(grad, 0, 1)
-        if bias_top is not None:
-            grad = jnp.concatenate([grad[:1] + bias_top[None], grad[1:]], axis=0)
-        if bias_bottom is not None:
-            grad = jnp.concatenate([grad[:-1], grad[-1:] + bias_bottom[None]], axis=0)
-        new_one, new_two, updated = adam(
-            grad.reshape(span, BLK),
-            p1[flat].reshape(span, BLK),
-            m1[flat].reshape(span, BLK),
-            m2[flat].reshape(span, BLK),
-        )
-        o1[at, :] = new_one
-        o2[at, :] = new_two
-        p2[at, :] = updated
-        return (updated * updated).reshape(rows_each, nb, BLK)
-
-    acc_ref[...] = jnp.sum(adam_rows(0, bias_top=bias_add[0]), axis=0)
-
-    @pl.loop(1, steps - 1)
-    def _(i):
-        acc_ref[...] = acc_ref[...] + jnp.sum(adam_rows(i), axis=0)
-
-    squares = adam_rows(steps - 1, bias_bottom=bias_add[1])
-    acc_main = acc_ref[...] + jnp.sum(squares[: rows_each - 1], axis=0)
-    acc_last = squares[rows_each - 1]
+    def edge_step(e):
+        return adam(gedge[e] + bias_add[e], edge_in[0, e], edge_in[1, e], edge_in[2, e])
+
+    edges = [edge_step(e) for e in range(2)]
+    acc_main = acc_ref[...] + edges[0][2] * edges[0][2]
+    acc_last = edges[1][2] * edges[1][2]
     ext_row = ext_ref[...]
     ext_row = jnp.where(par == 1, pltpu.roll(ext_row, 64, 1), ext_row)[7:8]
     ext_one, ext_two, ext_up = adam(
@@ -608,8 +611,18 @@
         target = fid((y + dy) % NY, zw(z + dz), (c + dc) % CORES)
         send(s_own, s_grp.at[i], s_sg, r_sg, x, target)
     finish_sums()
-    for write in writes:
-        write.start()
+    for n, (blocked, flat) in enumerate(((m1w, o1), (m2w, o2), (pw, p2))):
+
+        @pl.loop(0, BLK // rows_each)
+        def _(i):
+            some = blocked[:, pl.ds(pl.multiple_of(i * rows_each, rows_each), rows_each), :]
+            at = pl.ds(pl.multiple_of(i * span, span), span)
+            flat[at, :] = jnp.swapaxes(some, 0, 1).reshape(span, BLK)
+
+        flat[pl.ds(0, nb), :] = edges[0][n]
+        flat[pl.ds((BLK - 1) * nb, nb), :] = edges[1][n]
+        writes[n].start()
+
     arrive(s_grp, r_sg)
     sumsq = s_own[...] + jnp.sum(s_grp[...], axis=0)
     threshold = learn_rate * lasso_weight * math.sqrt(2 * HD * dim + HD)
@@ -733,7 +746,8 @@
     scratch = [
         vm((cells,)), vm((cells,)), vm((cells,)),
         vm((rows + 8, BLK)), vm((rows + 8, BLK)), vm((rows + 8, BLK)),
-        vm((nb, BLK, BLK)), vm((nb, BLK, BLK)), vm((nb, BLK, BLK)),
+        vm((nb, BLK, BLK)), vm((nb, BLK, BLK)), vm((nb, BLK, BLK)), vm((nb, BLK, BLK)),
+        vm((3, 2, nb, BLK)), vm((2, nb, BLK)),
         vm((NX, BLK, TOK), BF16), vm((NX, 16, TOK), BF16),
         vm((BLK + 32, TOK)), vm((2 * BLK, NX * TOK), BF16), vm((TOK, 2 * BLK), BF16),
         vm((nz, 2, 2 * BLK, NY // 2 * BLK), BF16), vm((NX, nz, NY, TOK, BLK), BF16),

time: 56.8 us -> 56 us (0.986)
  Pallas kernels: 54.4 us -> 53.5 us
    pallas_call x1, Pallas kernels: 51.6 us -> 50.8 us  [on_device(): pl.pallas_call(functools.partial(kernel, nz), grid=(1,), out_shape=[cotan...]
where the time goes in v5:
time: 56 us; the launch traced here: 55.8 us
  Pallas kernels  53.5 us (96%)
  between operations  1.37 us (2%)
  other arithmetic  0.86 us (2%)
    pallas_call x1, Pallas kernels, on_device(): pl.pallas_call(functools.partial(kernel, nz), grid=(1,), out_shape=[cotan...  50.8 us
    pallas_call x1, Pallas kernels, on_device(): pl.pallas_call(functools.partial(finish, nb), out_shape=[cotangent] * 2 +...  2.74 us

profile of v5, /device:TPU:1, one launch (start us, length us, event | category | flops | bytes accessed | tf_op | source)
XLA Modules:
  0.0 55.8 jit_solution(6698303637859057337)
XLA Ops:
  1.4 0.1 pad_maximum_fusion.1.fixes
  1.4 0.8 %pad_maximum_fusion.acts = bf16[4,64,128]{2,1,0:T(8,128)(2,1)S(1)} fusion(bf16[1,64,128]{2,1,0:T(8,128)(2,1)} %bitcast.20, bf16[1,64,128]{2,1,0:T(8,128)(2,1)} %bitcast.21, bf16[1,64,128]{2,1,0:T(8,128)(2,1)} %bitcast.22, bf16[1,64,128]{2,1,0:T(8,128)(2,1)} %bitcast.23), kind=kLoop, calls=%fused_computation | loop fusion | flops 98304 | bytes 131072 | tf_op jit(solution)/shard_map/stack | solution.py:788
  2.2 50.8 %step.1 = (bf16[64,128]{1,0:T(8,128)(2,1)S(1)}, bf16[64,128]{1,0:T(8,128)(2,1)S(1)}, f32[4104,128]{1,0:T(8,128)S(1)}, f32[4104,128]{1,0:T(8,128)S(1)}, f32[4104,128]{1,0:T(8,128)S(1)}, /*index=5*/f32[72,128]{1,0:T(8,128)S(1)}) custom-call(bf16[4,64,128]{2,1,0:T(8,128)(2,1)S(1)} %pad_maximum_fusion.acts, f32[524352]{0:T(1024)} %p_hbm.1, f32[524352]{0:T(1024)} %m1_hbm.1, ...), custom_call_target="tpu_custom_call" | custom-call | flops 1073741824 | bytes 12582912 | tf_op jit(solution)/shard_map/step/pallas_call | solution.py:769
  53.0 2.7 %finish.1 = (bf16[64,128]{1,0:T(8,128)(2,1)}, bf16[64,128]{1,0:T(8,128)(2,1)}, f32[4104,128]{1,0:T(8,128)}, f32[4104,128]{1,0:T(8,128)}, f32[4104,128]{1,0:T(8,128)}) custom-call(bf16[64,128]{1,0:T(8,128)(2,1)S(1)} %get-tuple-element.16.gh, bf16[64,128]{1,0:T(8,128)(2,1)S(1)} %get-tuple-element.17.ga, f32[4104,128]{1,0:T(8,128)S(1)} %get-tuple-element.18.up, ...), custom_call_target="tpu_custom_call" | custom-call | tf_op jit(solution)/shard_map/finish/pallas_call | solution.py:791

commit v6 on v5

--- a/solution.py
+++ b/solution.py
@@ -14,7 +14,6 @@
 CORES = 2
 TOK = 128
 BLK = 128
-DIRECT = 4
 
 beta_one = 0.9
 beta_two = 0.95
@@ -226,8 +225,6 @@
                 send_later(ref, ref, s_rz.at[2 * r + 2], r_rz.at[2 * r + 2], x, z_short)
             send_later(ref, ref, s_r1.at[idx, 0], r_r1.at[idx, 0], x_up, f)
             send_later(ref, ref, s_r1.at[idx, 1], r_r1.at[idx, 1], x_down, f)
-            if r >= DIRECT:
-                send_later(ref, ref, s_r2.at[idx, 0], r_r2.at[idx, 0], x_far, f)
             if r > 0:
                 send_later(ref, ref, s_rp.at[x, zq], r_rp.at[x, zq], x, partner)
 
@@ -236,9 +233,8 @@
             ways = ((x_down, x_up), (x_up, x_down))
             for way, (frm, to) in enumerate(ways):
                 arrive(rbuf.at[frm, zq, pair(c)], r_r1.at[idx, way])
-                if r < DIRECT:
-                    part = rbuf.at[frm, zq, half_y * c + way]
-                    send_later(part, part, s_r2.at[idx, way], r_r2.at[idx, way], to, f)
+                part = rbuf.at[frm, zq, half_y * c + way]
+                send_later(part, part, s_r2.at[idx, way], r_r2.at[idx, way], to, f)
             for frm, _ in ways:
                 ref = rbuf.at[frm, zq, pair(c)]
                 send_later(ref, ref, s_rp.at[frm, zq], r_rp.at[frm, zq], x, partner)
@@ -246,11 +242,8 @@
     def round_x2(r):
         for idx, zq in z_quad(r):
             ref = rbuf.at[x_far, zq, pair(c)]
-            if r < DIRECT:
-                for way in range(2):
-                    arrive(rbuf.at[x_far, zq, half_y * c + way], r_r2.at[idx, way])
-            else:
-                arrive(ref, r_r2.at[idx, 0])
+            for way in range(2):
+                arrive(rbuf.at[x_far, zq, half_y * c + way], r_r2.at[idx, way])
             send_later(ref, ref, s_rp.at[x_far, zq], r_rp.at[x_far, zq], x, partner)
 
     own_quad()

time: 56 us -> 55.1 us (0.984)
  Pallas kernels: 53.5 us -> 52.6 us
    pallas_call x1, Pallas kernels: 50.8 us -> 49.9 us  [on_device(): pl.pallas_call(functools.partial(kernel, nz), grid=(1,), out_shape=[cotan...]
where the time goes in v6:
time: 55.1 us; the launch traced here: 54.8 us
  Pallas kernels  52.6 us (95%)
  between operations  1.37 us (2%)
  other arithmetic  0.86 us (2%)
    pallas_call x1, Pallas kernels, on_device(): pl.pallas_call(functools.partial(kernel, nz), grid=(1,), out_shape=[cotan...  49.9 us
    pallas_call x1, Pallas kernels, on_device(): pl.pallas_call(functools.partial(finish, nb), out_shape=[cotangent] * 2 +...  2.74 us

profile of v6, /device:TPU:1, one launch (start us, length us, event | category | flops | bytes accessed | tf_op | source)
XLA Modules:
  0.0 54.8 jit_solution(11364282568899965038)
XLA Ops:
  1.4 0.1 pad_maximum_fusion.1.fixes
  1.4 0.8 %pad_maximum_fusion.acts = bf16[4,64,128]{2,1,0:T(8,128)(2,1)S(1)} fusion(bf16[1,64,128]{2,1,0:T(8,128)(2,1)} %bitcast.20, bf16[1,64,128]{2,1,0:T(8,128)(2,1)} %bitcast.21, bf16[1,64,128]{2,1,0:T(8,128)(2,1)} %bitcast.22, bf16[1,64,128]{2,1,0:T(8,128)(2,1)} %bitcast.23), kind=kLoop, calls=%fused_computation | loop fusion | flops 98304 | bytes 131072 | tf_op jit(solution)/shard_map/stack | solution.py:781
  2.2 49.9 %step.1 = (bf16[64,128]{1,0:T(8,128)(2,1)S(1)}, bf16[64,128]{1,0:T(8,128)(2,1)S(1)}, f32[4104,128]{1,0:T(8,128)S(1)}, f32[4104,128]{1,0:T(8,128)S(1)}, f32[4104,128]{1,0:T(8,128)S(1)}, /*index=5*/f32[72,128]{1,0:T(8,128)S(1)}) custom-call(bf16[4,64,128]{2,1,0:T(8,128)(2,1)S(1)} %pad_maximum_fusion.acts, f32[524352]{0:T(1024)} %p_hbm.1, f32[524352]{0:T(1024)} %m1_hbm.1, ...), custom_call_target="tpu_custom_call" | custom-call | flops 1073741824 | bytes 12582912 | tf_op jit(solution)/shard_map/step/pallas_call | solution.py:762
  52.1 2.7 %finish.1 = (bf16[64,128]{1,0:T(8,128)(2,1)}, bf16[64,128]{1,0:T(8,128)(2,1)}, f32[4104,128]{1,0:T(8,128)}, f32[4104,128]{1,0:T(8,128)}, f32[4104,128]{1,0:T(8,128)}) custom-call(bf16[64,128]{1,0:T(8,128)(2,1)S(1)} %get-tuple-element.16.gh, bf16[64,128]{1,0:T(8,128)(2,1)S(1)} %get-tuple-element.17.ga, f32[4104,128]{1,0:T(8,128)S(1)} %get-tuple-element.18.up, ...), custom_call_target="tpu_custom_call" | custom-call | tf_op jit(solution)/shard_map/finish/pallas_call | solution.py:784
